TPU v7x, 128 devices: a whole 4x4x4 slice. The times are simulated.
128 devices in a mesh: aux: 32 (over x, z, core), orb: 4 (over y).
Axes of the slice: x: 4, y: 4, z: 4, core: 2. Of those that a mesh axis runs over, the one named last changes fastest.
Arguments:
- three_centre: bfloat16 [512, 512, 2048], P('orb', 'aux'), may hold values from -6 to 6
- pair_mask: int32 [4, 4], replicated, may hold values 0 or 1
- aux_mask: int32 [4, 16], replicated, may hold values 0 or 1
- density: bfloat16 [512, 1024], P('orb', 'aux'), may hold values from -0.25 to 0.25
Outputs:
- contracted: bfloat16 [2048, 512, 1024], P('aux', 'orb')
All inputs are finite; a program needn't handle non-finite values.
Results may differ from a plain program's by a relative error of at most 0.001.
Values may be sent and summed in bfloat16 or wider, within the bound.
No kernel may reach another device: no remote copies, remote signals or barrier semaphores. Data moves between devices by JAX's collectives and lax.ppermute only.
A program may use at most 128 MiB of HBM per device.

v0:
```python
import jax
import jax.numpy as jnp
from jax import lax
from jax.sharding import PartitionSpec as P

BLK = 128


def one_hot(global_rows, count):
    blocks = global_rows // BLK
    return (blocks[:, None] == jnp.arange(count, dtype=jnp.int32)[None, :]).astype(jnp.float32)


def pair_table(pair_mask, orb_pos, mub_local, nu_rows):
    own = lax.dynamic_slice_in_dim(pair_mask, orb_pos * mub_local, mub_local, 0)
    return jnp.dot(own.astype(jnp.float32), one_hot(nu_rows, pair_mask.shape[1]).T)


def aux_table(aux_mask, nu_rows, p_rows):
    left = jnp.dot(one_hot(nu_rows, aux_mask.shape[0]), aux_mask.astype(jnp.float32))
    return jnp.dot(left, one_hot(p_rows, aux_mask.shape[1]).T)


def apply_masks(data, pair_part, aux_part):
    mu_count, nu_count, p_count = data.shape
    mub_local = mu_count // BLK
    shaped = data.reshape(mub_local, BLK, nu_count, p_count)
    keep = pair_part[:, None, :, None] * aux_part[None, None, :, :] > 0.5
    kept = jnp.where(keep, shaped, jnp.zeros((), jnp.bfloat16))
    return kept.reshape(mu_count, nu_count, p_count)


def local(three_centre, pair_mask, aux_mask, density):
    mu_count, nu_local, p_total = three_centre.shape
    aux_pos = lax.axis_index("aux")
    orb_pos = lax.axis_index("orb")
    aux_count = lax.axis_size("aux")
    p_local = p_total // aux_count
    mub_local = mu_count // BLK
    nu_all = jnp.arange(nu_local * aux_count, dtype=jnp.int32)
    p_mine = aux_pos * p_local + jnp.arange(p_local, dtype=jnp.int32)
    dens_rows = lax.all_gather(density, "orb", axis=0, tiled=True)
    dens_whole = lax.all_gather(dens_rows, "aux", axis=1, tiled=True)
    moved = lax.all_to_all(three_centre, "aux", split_axis=2, concat_axis=1, tiled=True)
    pair_dest = pair_table(pair_mask, orb_pos, mub_local, nu_all)
    relaid = apply_masks(moved, pair_dest, aux_table(aux_mask, nu_all, p_mine))
    return jnp.einsum("mnp,ns->pms", relaid, dens_whole, preferred_element_type=jnp.float32).astype(
        jnp.bfloat16
    )


def solution(mesh):
    in_specs = (P("orb", "aux", None), P(), P(), P("orb", "aux"))
    out_specs = P("aux", "orb", None)
    return jax.shard_map(local, mesh=mesh, in_specs=in_specs, out_specs=out_specs, check_vma=False)
```

profile of v0, /device:TPU:60, one launch (start us, length us, event | category | flops | bytes accessed | tf_op | source)
XLA Modules:
  0.0 199.0 jit_solution(1949138777017401225)
XLA Ops:
  6.5 13.3 %copy.10 = bf16[128,16,2048]{0,1,2:T(8,128)(2,1)} copy(bf16[128,16,2048]{2,1,0:T(8,128)(2,1)} %param.4) | data formatting | bytes 16777216 | tf_op args[0]
  19.9 0.0 copy-start
  19.9 0.0 copy-start.1
  19.9 8.2 %all-to-all-start = ((bf16[128,16,2048]{0,1,2:T(8,128)(2,1)}), bf16[128,16,2048]{0,1,2:T(8,128)(2,1)}, u32[]{:S(2)}, u32[]{:S(2)}) async-start(bf16[128,16,2048]{0,1,2:T(8,128)(2,1)} %copy.10), calls=%async_computation | async-start | bytes 16777216 | tf_op jit(solution)/shard_map/all_to_all | solution.py:44
  28.0 0.0 all-gather.2.cloned.1.call-start
  28.1 0.0 copy-done
  28.1 10.8 %all_gather.6 = bf16[512,32]{0,1:T(8,128)(2,1)} all-gather(bf16[128,32]{0,1:T(8,128)(2,1)S(1)} %copy-done), channel_id=1, replica_groups=mesh['aux'=32,'orb'=4] {'orb'}, dimensions={0}, use_global_device_ids=true | all-gather | bytes 40960 | tf_op jit(solution)/shard_map/all_gather | solution.py:42
  38.9 0.0 all-gather.2.cloned.1.call-update
  38.9 0.9 fusion.5
  39.9 0.0 copy-done.1
  39.9 0.4 fusion.1
  40.3 0.2 copy.9
  40.5 114.9 %all-to-all-done = bf16[128,16,2048]{0,1,2:T(8,128)(2,1)} async-done(((bf16[128,16,2048]{0,1,2:T(8,128)(2,1)}), bf16[128,16,2048]{0,1,2:T(8,128)(2,1)}, u32[]{:S(2)}, u32[]{:S(2)}) %all-to-all-start) | async-done | bytes 8388640 | tf_op jit(solution)/shard_map/all_to_all | solution.py:44
  155.3 8.9 %copy.12 = bf16[128,32,16,64]{0,3,2,1:T(8,128)(2,1)} copy(bf16[128,32,16,64]{0,2,3,1:T(8,128)(2,1)} %bitcast.5) | data formatting | bytes 16777216 | tf_op jit(solution)/shard_map/all_to_all | solution.py:44
  164.3 7.7 %bitcast_select_fusion = bf16[128,512,64]{0,2,1:T(8,128)(2,1)} fusion(bf16[128,32,16,64]{0,3,2,1:T(8,128)(2,1)} %copy.12, pred[512,64]{1,0:T(8,128)(4,1)S(1)} %copy.9), kind=kLoop, calls=%fused_computation.1 | loop fusion | flops 4194304 | bytes 16809984 | tf_op jit(solution)/shard_map/jit(_where)/select_n | solution.py:29
  172.0 0.0 all-gather.2.cloned.1.call-done
  172.0 20.2 %convert_bitcast_fusion = bf16[64,128,1024]{2,1,0:T(8,128)(2,1)} fusion(bf16[128,512,64]{0,2,1:T(8,128)(2,1)} %bitcast_select_fusion, bf16[512,1024]{0,1:T(8,128)(2,1)} %all-gather.2.cloned.1.call-done), kind=kOutput, calls=%fused_computation | convolution fusion | flops 8598323200 | bytes 26214400 | tf_op jit(solution)/shard_map/mnp,ns->pms/dot_general | solution.py:47
  (2 shorter events, 0.0 us)
Async XLA Ops:
  19.9 8.2 %copy-start = (bf16[128,32]{0,1:T(8,128)(2,1)S(1)}, bf16[128,32]{0,1:T(8,128)(2,1)}, u32[]{:S(2)}) copy-start(bf16[128,32]{0,1:T(8,128)(2,1)} %param.7) | copy-start | bytes 24580
  19.9 20.0 %copy-start.1 = (s32[4,16]{1,0:T(4,128)S(1)}, s32[4,16]{1,0:T(4,128)}, u32[]{:S(2)}) copy-start(s32[4,16]{1,0:T(4,128)} %param.6) | copy-start | bytes 772
  19.9 135.5 %all-to-all-start = ((bf16[128,16,2048]{0,1,2:T(8,128)(2,1)}), bf16[128,16,2048]{0,1,2:T(8,128)(2,1)}, u32[]{:S(2)}, u32[]{:S(2)}) async-start(bf16[128,16,2048]{0,1,2:T(8,128)(2,1)} %copy.10), calls=%async_computation | async-start | bytes 16777216 | tf_op jit(solution)/shard_map/all_to_all | solution.py:44
  28.0 143.9 %all-gather.2.cloned.1.call-start = ((), (), s32[]{:S(2)}) async-start(), calls=%async_computation.1 | async-start | bytes 1081344 | tf_op jit(solution)/shard_map/all_gather | solution.py:43
Sparse Core Ops, SparseCore 0:
  39.0 95.0 all-gather.1
where the time goes:
time: 200 us; the launch traced here: 199 us
  waiting for transfers between devices  115 us (58%)
  local copies, waits for them, and re-layouts  22.4 us (11%)
  matrix products  21.5 us (11%)
  between operations  13.4 us (7%)
  blocking collectives  10.8 us (5%)
  starting transfers between devices  8.22 us (4%)
  other arithmetic  7.71 us (4%)
    all_to_all x1, waiting for transfers between devices, local(): lax.all_to_all(three_centre, 'aux', split_axis=2, concat_axis=1, tiled=True)  115 us
    dot_general x1, matrix products, local(): jnp.einsum('mnp,ns->pms', relaid, dens_whole, preferred_element_type=jnp....  20.2 us
    unnamed x5, local copies, waits for them, and re-layouts  13.3 us
    all_gather x1, blocking collectives, local(): dens_rows = lax.all_gather(density, 'orb', axis=0, tiled=True)  10.8 us
    all_to_all x1, local copies, waits for them, and re-layouts, local(): lax.all_to_all(three_centre, 'aux', split_axis=2, concat_axis=1, tiled=True)  8.94 us
    all_to_all x1, starting transfers between devices, local(): lax.all_to_all(three_centre, 'aux', split_axis=2, concat_axis=1, tiled=True)  8.17 us
    select_n x1, other arithmetic, apply_masks(): kept = jnp.where(keep, shaped, jnp.zeros((), jnp.bfloat16))  7.7 us
  transfers between devices with their start and end apart: 2, of which 1 were waited for; matrix products, arithmetic and copies ran while one was open for 9% of the time, Pallas kernels for 0%

commit v1 on v0

v1 whole, which is shorter than its diff:
```python
import jax
import jax.numpy as jnp
from jax import lax
from jax.experimental import pallas as pl
from jax.experimental.pallas import tpu as pltpu
from jax.sharding import PartitionSpec as P

BLK = 128
P_STEP = 8


def swap_bit(part, axis, bit):
    count = lax.axis_size(axis)
    other = lax.ppermute(part, axis, [(i, i ^ bit) for i in range(count)])
    upper = (lax.axis_index(axis) & bit) != 0
    return jnp.stack([jnp.where(upper, other, part), jnp.where(upper, part, other)])


def gather_density(density):
    part = density.T
    for axis, bit in (("aux", 8), ("aux", 16), ("aux", 2), ("aux", 4), ("orb", 1), ("orb", 2), ("aux", 1)):
        part = swap_bit(part, axis, bit)
    whole = jnp.transpose(part, (1, 2, 8, 5, 6, 3, 4, 0, 7))
    return whole.reshape(4 * density.shape[0], 32 * density.shape[1])


def contract_kernel(x_ref, d_ref, o_ref):
    sources, step, nu, mu = x_ref.shape
    dens = d_ref[...]
    for p in range(step):
        rows = x_ref[:, p].reshape(sources * nu, mu)
        o_ref[p] = lax.dot_general(
            rows, dens, (((0,), (0,)), ((), ())), preferred_element_type=jnp.float32
        ).astype(jnp.bfloat16)


def contract(moved, dens):
    sources, p_local, nu, mu = moved.shape
    nu_all, sig = dens.shape
    return pl.pallas_call(
        contract_kernel,
        out_shape=jax.ShapeDtypeStruct((p_local, mu, sig), jnp.bfloat16),
        grid=(p_local // P_STEP,),
        in_specs=[
            pl.BlockSpec((sources, P_STEP, nu, mu), lambda i: (0, i, 0, 0)),
            pl.BlockSpec((nu_all, sig), lambda i: (0, 0)),
        ],
        out_specs=pl.BlockSpec((P_STEP, mu, sig), lambda i: (i, 0, 0)),
        compiler_params=pltpu.CompilerParams(vmem_limit_bytes=48 << 20),
        cost_estimate=pl.CostEstimate(
            flops=2 * p_local * mu * nu_all * sig, bytes_accessed=26 << 20, transcendentals=0
        ),
    )(moved, dens)


def local(three_centre, pair_mask, aux_mask, density):
    mu, nu, p_total = three_centre.shape
    aux_pos, orb_pos, aux_count = lax.axis_index("aux"), lax.axis_index("orb"), lax.axis_size("aux")
    p_local = p_total // aux_count
    sent = jnp.transpose(three_centre, (2, 1, 0)).reshape(aux_count, p_local, nu, mu)
    moved = lax.all_to_all(sent, "aux", split_axis=0, concat_axis=0, tiled=True)
    pair = lax.dynamic_index_in_dim(pair_mask, orb_pos, 0, keepdims=False)
    aux = lax.dynamic_index_in_dim(aux_mask, aux_pos * p_local // BLK, 1, keepdims=False)
    keep = jnp.repeat(pair * aux, BLK).astype(jnp.bfloat16)
    dens = gather_density(density) * keep[:, None]
    return contract(moved, dens)


def solution(mesh):
    in_specs = (P("orb", "aux", None), P(), P(), P("orb", "aux"))
    out_specs = P("aux", "orb", None)
    return jax.shard_map(local, mesh=mesh, in_specs=in_specs, out_specs=out_specs, check_vma=False)
```

time: 200 us -> 196 us (0.980)
  the two profiles are of different devices: /device:TPU:60 before, /device:TPU:1 now
where the time goes in v1:
time: 196 us; the launch traced here: 195 us
  waiting for transfers between devices  126 us (64%)
  starting transfers between devices  37 us (19%)
  local copies, waits for them, and re-layouts  15.7 us (8%)
  Pallas kernels  15.3 us (8%)
    ppermute x7, waiting for transfers between devices, swap_bit(): other = lax.ppermute(part, axis, [(i, i ^ bit) for i in range(count)])  126 us
    ppermute x7, starting transfers between devices, swap_bit(): other = lax.ppermute(part, axis, [(i, i ^ bit) for i in range(count)])  27.4 us
    pallas_call x1, Pallas kernels, contract(): pl.pallas_call(contract_kernel, out_shape=jax.ShapeDtypeStruct((p_local,...  15.3 us
    transpose x1, local copies, waits for them, and re-layouts, local(): jnp.transpose(three_centre, (2, 1, 0)).reshape(aux_count, p_local, nu, mu)  13.3 us
    all_to_all x1, starting transfers between devices, local(): moved = lax.all_to_all(sent, 'aux', split_axis=0, concat_axis=0, tiled=True)  9.62 us
  transfers between devices with their start and end apart: 8, of which 7 were waited for; matrix products, arithmetic and copies ran while one was open for 2% of the time, Pallas kernels for 0%

profile of v1, /device:TPU:1, one launch (start us, length us, event | category | flops | bytes accessed | tf_op | source)
XLA Modules:
  0.0 195.0 jit_solution(18253365741835981928)
XLA Ops:
  0.0 0.0 copy-start
  0.0 13.3 %copy.7 = bf16[2048,16,128]{2,1,0:T(8,128)(2,1)} copy(bf16[2048,16,128]{0,1,2:T(8,128)(2,1)} %bitcast.44) | data formatting | bytes 16777216 | tf_op jit(solution)/shard_map/transpose | solution.py:60
  13.3 0.0 copy-start.1
  13.3 9.6 %all-to-all-start = ((bf16[32,64,16,128]{3,2,1,0:T(8,128)(2,1)}), bf16[32,64,16,128]{3,2,1,0:T(8,128)(2,1)}, u32[]{:S(2)}, u32[]{:S(2)}) async-start(bf16[32,64,16,128]{3,2,1,0:T(8,128)(2,1)} %bitcast.43), calls=%async_computation | async-start | bytes 16777216 | tf_op jit(solution)/shard_map/all_to_all | solution.py:61
  23.0 0.0 copy-done.1
  23.0 1.5 collective-permute-start
  24.4 107.1 %collective-permute-done = bf16[32,128]{1,0:T(8,128)(2,1)S(1)} collective-permute-done((bf16[32,128]{1,0:T(8,128)(2,1)S(1)}, bf16[32,128]{1,0:T(8,128)(2,1)S(1)}, u32[]{:S(2)}, u32[]{:S(2)}) %collective-permute-start) | collective-permute-done | bytes 8224 | tf_op jit(solution)/shard_map/ppermute | solution.py:14
  131.6 0.1 collective-permute-start.1
  131.7 4.5 %collective-permute-done.1 = bf16[2,32,128]{2,1,0:T(8,128)(2,1)S(1)} collective-permute-done((bf16[2,32,128]{2,1,0:T(8,128)(2,1)S(1)}, bf16[2,32,128]{2,1,0:T(8,128)(2,1)S(1)}, u32[]{:S(2)}, u32[]{:S(2)}) %collective-permute-start.1) | collective-permute-done | bytes 16416 | tf_op jit(solution)/shard_map/ppermute | solution.py:14
  136.2 15.1 %collective-permute-start.2 = (bf16[2,2,32,128]{3,2,1,0:T(8,128)(2,1)S(1)}, bf16[2,2,32,128]{3,2,1,0:T(8,128)(2,1)S(1)}, u32[]{:S(2)}, u32[]{:S(2)}) collective-permute-start(bf16[2,2,32,128]{3,2,1,0:T(8,128)(2,1)S(1)} %pad_maximum_fusion.4), channel_id=1, source_target_pairs={{0,8},{4,12},{8,0},{12,4},{16,24},{20,28},{24,16},{28,20},{32,40},... | collective-permute-start | bytes 98312 | tf_op jit(solution)/shard_map/ppermute | solution.py:14
  151.3 1.3 collective-permute-done.2
  152.6 0.1 collective-permute-start.3
  152.7 4.6 %collective-permute-done.3 = bf16[2,2,2,32,128]{4,3,2,1,0:T(8,128)(2,1)S(1)} collective-permute-done((bf16[2,2,2,32,128]{4,3,2,1,0:T(8,128)(2,1)S(1)}, bf16[2,2,2,32,128]{4,3,2,1,0:T(8,128)(2,1)S(1)}, u32[]{:S(2)}, u32[]{:S(2)}) %collective-permute-start.3) | collective-permute-done | bytes 65568 | tf_op jit(solution)/shard_map/ppermute | solution.py:14
  157.4 1.4 collective-permute-start.4
  158.7 2.5 %collective-permute-done.4 = bf16[2,2,2,2,32,128]{5,4,3,2,1,0:T(8,128)(2,1)S(1)} collective-permute-done((bf16[2,2,2,2,32,128]{5,4,3,2,1,0:T(8,128)(2,1)S(1)}, bf16[2,2,2,2,32,128]{5,4,3,2,1,0:T(8,128)(2,1)S(1)}, u32[]{:S(2)}, u32[]{:S(2)}) %collective-permute-start.4) | collective-permute-done | bytes 131104 | tf_op jit(solution)/shard_map/ppermute | solution.py:14
  161.3 3.0 %collective-permute-start.5 = (bf16[2,2,2,2,2,32,128]{6,5,4,3,2,1,0:T(8,128)(2,1)S(1)}, bf16[2,2,2,2,2,32,128]{6,5,4,3,2,1,0:T(8,128)(2,1)S(1)}, u32[]{:S(2)}, u32[]{:S(2)}) collective-permute-start(bf16[2,2,2,2,2,32,128]{6,5,4,3,2,1,0:T(8,128)(2,1)S(1)} %pad_maximum_fusion.1), channel_id=1, source_target_pairs={{0,2},{1,3},{2,0},{3,1},{4,6},{5,7},{6,4},{7,5},{8,10},{9,11},{10,... | collective-permute-start | bytes 786440 | tf_op jit(solution)/shard_map/ppermute | solution.py:14
  164.3 5.0 %collective-permute-done.5 = bf16[2,2,2,2,2,32,128]{6,5,4,3,2,1,0:T(8,128)(2,1)S(1)} collective-permute-done((bf16[2,2,2,2,2,32,128]{6,5,4,3,2,1,0:T(8,128)(2,1)S(1)}, bf16[2,2,2,2,2,32,128]{6,5,4,3,2,1,0:T(8,128)(2,1)S(1)}, u32[]{:S(2)}, u32[]{:S(2)}) %collective-permute-start.5) | collective-permute-done | bytes 262176 | tf_op jit(solution)/shard_map/ppermute | solution.py:14
  169.4 0.1 pad_maximum_fusion
  169.5 6.3 %collective-permute-start.6 = (bf16[2,2,2,2,2,2,32,128]{7,6,5,4,3,2,1,0:T(8,128)(2,1)S(1)}, bf16[2,2,2,2,2,2,32,128]{7,6,5,4,3,2,1,0:T(8,128)(2,1)S(1)}, u32[]{:S(2)}, u32[]{:S(2)}) collective-permute-start(bf16[2,2,2,2,2,2,32,128]{7,6,5,4,3,2,1,0:T(8,128)(2,1)S(1)} %pad_maximum_fusion), channel_id=1, source_target_pairs={{0,4},{4,0},{8,12},{12,8},{16,20},{20,16},{24,28},{28,24},{32,36},... | collective-permute-start | bytes 1572872 | tf_op jit(solution)/shard_map/ppermute | solution.py:14
  175.7 0.0 copy-done
  175.7 0.2 dynamic-slice_reduce_fusion
  175.9 0.7 fusion
  176.6 0.1 broadcast_bitcast_fusion
  176.7 0.6 collective-permute-done.6
  177.3 0.1 select_bitcast_fusion.1
  177.3 0.1 maximum_bitcast_fusion
  177.5 1.1 copy.8
  178.5 0.4 reshape.14
  179.0 0.5 copy.9
  179.5 0.1 broadcast_multiply_fusion.d_ref
  179.7 0.0 all-to-all-done.x_ref
  179.7 15.3 %shard_map.46 = bf16[64,128,1024]{2,1,0:T(8,128)(2,1)} custom-call(bf16[32,64,16,128]{3,2,1,0:T(8,128)(2,1)} %all-to-all-done.x_ref, bf16[512,1024]{1,0:T(8,128)(2,1)S(1)} %broadcast_multiply_fusion.d_ref), custom_call_target="tpu_custom_call" | custom-call | flops 8589934592 | bytes 27262976 | tf_op jit(solution)/shard_map/pallas_call | solution.py:40
  (11 shorter events, 0.2 us)
Async XLA Ops:
  0.0 175.7 %copy-start = (s32[4,16]{1,0:T(4,128)S(1)}, s32[4,16]{1,0:T(4,128)}, u32[]{:S(2)}) copy-start(s32[4,16]{1,0:T(4,128)} %param.6) | copy-start | bytes 772
  13.3 9.6 %copy-start.1 = (bf16[128,32]{0,1:T(8,128)(2,1)S(1)}, bf16[128,32]{0,1:T(8,128)(2,1)}, u32[]{:S(2)}) copy-start(bf16[128,32]{0,1:T(8,128)(2,1)} %param.7) | copy-start | bytes 24580
  13.3 166.3 %all-to-all-start = ((bf16[32,64,16,128]{3,2,1,0:T(8,128)(2,1)}), bf16[32,64,16,128]{3,2,1,0:T(8,128)(2,1)}, u32[]{:S(2)}, u32[]{:S(2)}) async-start(bf16[32,64,16,128]{3,2,1,0:T(8,128)(2,1)} %bitcast.43), calls=%async_computation | async-start | bytes 16777216 | tf_op jit(solution)/shard_map/all_to_all | solution.py:61
  23.0 108.6 %collective-permute-start = (bf16[32,128]{1,0:T(8,128)(2,1)S(1)}, bf16[32,128]{1,0:T(8,128)(2,1)S(1)}, u32[]{:S(2)}, u32[]{:S(2)}) collective-permute-start(bf16[32,128]{1,0:T(8,128)(2,1)S(1)} %bitcast.45), channel_id=1, source_target_pairs={{0,32},{4,36},{8,40},{12,44},{16,48},{20,52},{24,56},{28,60},{32,0... | collective-permute-start | bytes 24584 | tf_op jit(solution)/shard_map/ppermute | solution.py:14
  131.6 4.6 %collective-permute-start.1 = (bf16[2,32,128]{2,1,0:T(8,128)(2,1)S(1)}, bf16[2,32,128]{2,1,0:T(8,128)(2,1)S(1)}, u32[]{:S(2)}, u32[]{:S(2)}) collective-permute-start(bf16[2,32,128]{2,1,0:T(8,128)(2,1)S(1)} %pad_maximum_fusion.5), channel_id=1, source_target_pairs={{0,64},{4,68},{8,72},{12,76},{16,80},{20,84},{24,88},{28,92},{32,9... | collective-permute-start | bytes 49160 | tf_op jit(solution)/shard_map/ppermute | solution.py:14
  136.2 16.4 %collective-permute-start.2 = (bf16[2,2,32,128]{3,2,1,0:T(8,128)(2,1)S(1)}, bf16[2,2,32,128]{3,2,1,0:T(8,128)(2,1)S(1)}, u32[]{:S(2)}, u32[]{:S(2)}) collective-permute-start(bf16[2,2,32,128]{3,2,1,0:T(8,128)(2,1)S(1)} %pad_maximum_fusion.4), channel_id=1, source_target_pairs={{0,8},{4,12},{8,0},{12,4},{16,24},{20,28},{24,16},{28,20},{32,40},... | collective-permute-start | bytes 98312 | tf_op jit(solution)/shard_map/ppermute | solution.py:14
  152.6 4.7 %collective-permute-start.3 = (bf16[2,2,2,32,128]{4,3,2,1,0:T(8,128)(2,1)S(1)}, bf16[2,2,2,32,128]{4,3,2,1,0:T(8,128)(2,1)S(1)}, u32[]{:S(2)}, u32[]{:S(2)}) collective-permute-start(bf16[2,2,2,32,128]{4,3,2,1,0:T(8,128)(2,1)S(1)} %pad_maximum_fusion.3), channel_id=1, source_target_pairs={{0,16},{4,20},{8,24},{12,28},{16,0},{20,4},{24,8},{28,12},{32,48},... | collective-permute-start | bytes 196616 | tf_op jit(solution)/shard_map/ppermute | solution.py:14
  157.4 3.9 %collective-permute-start.4 = (bf16[2,2,2,2,32,128]{5,4,3,2,1,0:T(8,128)(2,1)S(1)}, bf16[2,2,2,2,32,128]{5,4,3,2,1,0:T(8,128)(2,1)S(1)}, u32[]{:S(2)}, u32[]{:S(2)}) collective-permute-start(bf16[2,2,2,2,32,128]{5,4,3,2,1,0:T(8,128)(2,1)S(1)} %pad_maximum_fusion.2), channel_id=1, source_target_pairs={{0,1},{1,0},{2,3},{3,2},{4,5},{5,4},{6,7},{7,6},{8,9},{9,8},{10,11... | collective-permute-start | bytes 393224 | tf_op jit(solution)/shard_map/ppermute | solution.py:14
  161.3 8.0 %collective-permute-start.5 = (bf16[2,2,2,2,2,32,128]{6,5,4,3,2,1,0:T(8,128)(2,1)S(1)}, bf16[2,2,2,2,2,32,128]{6,5,4,3,2,1,0:T(8,128)(2,1)S(1)}, u32[]{:S(2)}, u32[]{:S(2)}) collective-permute-start(bf16[2,2,2,2,2,32,128]{6,5,4,3,2,1,0:T(8,128)(2,1)S(1)} %pad_maximum_fusion.1), channel_id=1, source_target_pairs={{0,2},{1,3},{2,0},{3,1},{4,6},{5,7},{6,4},{7,5},{8,10},{9,11},{10,... | collective-permute-start | bytes 786440 | tf_op jit(solution)/shard_map/ppermute | solution.py:14
  169.5 7.8 %collective-permute-start.6 = (bf16[2,2,2,2,2,2,32,128]{7,6,5,4,3,2,1,0:T(8,128)(2,1)S(1)}, bf16[2,2,2,2,2,2,32,128]{7,6,5,4,3,2,1,0:T(8,128)(2,1)S(1)}, u32[]{:S(2)}, u32[]{:S(2)}) collective-permute-start(bf16[2,2,2,2,2,2,32,128]{7,6,5,4,3,2,1,0:T(8,128)(2,1)S(1)} %pad_maximum_fusion), channel_id=1, source_target_pairs={{0,4},{4,0},{8,12},{12,8},{16,20},{20,16},{24,28},{28,24},{32,36},... | collective-permute-start | bytes 1572872 | tf_op jit(solution)/shard_map/ppermute | solution.py:14

commit v2 on v1

v2 whole, which is shorter than its diff:
```python
import jax
import jax.numpy as jnp
from jax import lax
from jax.experimental import pallas as pl
from jax.experimental.pallas import tpu as pltpu
from jax.sharding import PartitionSpec as P

BLK = 128
LANES = 128
HALF = 64
GROUP = 16
PAIRS = 8
PITCH = 24
VMEM = 60 << 20


def swap_bit(part, axis, bit):
    count = lax.axis_size(axis)
    other = lax.ppermute(part, axis, [(i, i ^ bit) for i in range(count)])
    upper = (lax.axis_index(axis) & bit) != 0
    return jnp.stack([jnp.where(upper, other, part), jnp.where(upper, part, other)])


def pack_kernel(x_ref, *rest):
    o_ref = rest[-1]
    for group in range(x_ref.shape[0] // GROUP):
        top = group * GROUP
        for block in range(x_ref.shape[2] // LANES):
            lanes = slice(block * LANES, (block + 1) * LANES)
            low, high = x_ref[top : top + PAIRS, :, lanes], x_ref[top + PAIRS : top + GROUP, :, lanes]
            rows = slice(group * PAIRS, (group + 1) * PAIRS)
            o_ref[2 * block, rows] = jnp.concatenate([low[..., :HALF], high[..., :HALF]], axis=-1)
            o_ref[2 * block + 1, rows] = jnp.concatenate([low[..., HALF:], high[..., HALF:]], axis=-1)


def pack(three_centre, first, count, rows, extra, earlier=None):
    mu, nu, p_total = three_centre.shape
    targets = p_total // HALF
    args, specs, aliases = [three_centre], [pl.BlockSpec((rows, nu, p_total), lambda i: (first + i, 0, 0))], {}
    if earlier is not None:
        args, specs, aliases = args + [earlier], specs + [pl.BlockSpec(memory_space=pl.ANY)], {1: 0}
    return pl.pallas_call(
        pack_kernel,
        out_shape=jax.ShapeDtypeStruct((targets, mu // 2 + extra, nu, LANES), jnp.bfloat16),
        grid=(count,),
        in_specs=specs,
        out_specs=pl.BlockSpec((targets, rows // 2, nu, LANES), lambda i: (0, first + i, 0, 0)),
        input_output_aliases=aliases,
        compiler_params=pltpu.CompilerParams(vmem_limit_bytes=VMEM),
        cost_estimate=pl.CostEstimate(
            flops=0, bytes_accessed=4 * count * rows * nu * p_total, transcendentals=0
        ),
    )(*args)


def append_kernel(d_ref, sent_ref, o_ref):
    half = d_ref.shape[1] // 2
    for target in range(o_ref.shape[0]):
        core = target % 2
        o_ref[target] = d_ref[:, core * half : (core + 1) * half]


def append(sent, columns):
    targets, rows, nu, lanes = sent.shape
    orbs = columns.shape[0]
    return pl.pallas_call(
        append_kernel,
        out_shape=jax.ShapeDtypeStruct(sent.shape, sent.dtype),
        grid=(1,),
        in_specs=[pl.BlockSpec(columns.shape, lambda i: (0, 0, 0)), pl.BlockSpec(memory_space=pl.ANY)],
        out_specs=pl.BlockSpec((targets, orbs, nu, lanes), lambda i: (0, rows // orbs - 1, 0, 0)),
        input_output_aliases={1: 0},
        compiler_params=pltpu.CompilerParams(vmem_limit_bytes=VMEM),
    )(columns, sent)


def contract_kernel(keep_ref, x_ref, mine_ref, other_ref, o_ref, dens_ref, rows_ref):
    sources, _, nu, _ = x_ref.shape
    depth = sources * nu
    _, orbs, half, lanes = mine_ref.shape

    @pl.when(pl.program_id(0) == 0)
    def _():
        upper = keep_ref[orbs] == 1
        for orb in range(orbs):
            keep = keep_ref[orb].astype(jnp.float32).astype(jnp.bfloat16)
            mine, other = mine_ref[:, orb], other_ref[:, orb]
            low, high = jnp.where(upper, other, mine), jnp.where(upper, mine, other)
            whole = jnp.stack([low, high], axis=1).reshape(sources * 2 * half, lanes)
            dens_ref[orb * lanes : (orb + 1) * lanes, :] = whole.T * keep

    for pair in range(PAIRS):
        turned = x_ref[:, pair].reshape(depth, LANES).T.astype(jnp.float32)
        for k in range(depth // LANES):
            piece = turned[:, k * LANES : (k + 1) * LANES]
            base = k * HALF * PITCH + pair
            rows_ref[pl.ds(base, HALF, stride=PITCH), :] = piece[:HALF]
            rows_ref[pl.ds(base + PAIRS, HALF, stride=PITCH), :] = piece[HALF:]
    pieces = []
    for k in range(depth // LANES):
        piece = rows_ref[k * HALF * PITCH : (k + 1) * HALF * PITCH, :].reshape(HALF, PITCH, LANES)
        pieces.append(piece[:, :GROUP].reshape(HALF * GROUP, LANES).astype(jnp.bfloat16))
    product = jnp.dot(jnp.concatenate(pieces, axis=1), dens_ref[...], preferred_element_type=jnp.float32)
    o_ref[...] = product.astype(jnp.bfloat16).reshape(o_ref.shape)


def contract(moved, other, keep):
    sources, orbs, nu, _ = other.shape
    pairs = moved.shape[1] - orbs
    sig = sources * 2 * nu
    return pl.pallas_call(
        contract_kernel,
        out_shape=jax.ShapeDtypeStruct((HALF, 2 * pairs, sig), jnp.bfloat16),
        grid=(pairs // PAIRS,),
        in_specs=[
            pl.BlockSpec(memory_space=pltpu.SMEM),
            pl.BlockSpec((sources, PAIRS, nu, LANES), lambda i: (0, i, 0, 0)),
            pl.BlockSpec((sources, orbs, nu, LANES), lambda i: (0, pairs // orbs, 0, 0)),
            pl.BlockSpec(other.shape, lambda i: (0, 0, 0, 0)),
        ],
        out_specs=pl.BlockSpec((HALF, GROUP, sig), lambda i: (0, i, 0)),
        scratch_shapes=[
            pltpu.VMEM((orbs * LANES, sig), jnp.bfloat16),
            pltpu.VMEM((orbs * HALF * PITCH, LANES), jnp.float32),
        ],
        compiler_params=pltpu.CompilerParams(vmem_limit_bytes=VMEM),
        cost_estimate=pl.CostEstimate(
            flops=4 * HALF * pairs * orbs * LANES * sig, bytes_accessed=26 << 20, transcendentals=0
        ),
    )(keep, moved, moved, other)


def local(three_centre, pair_mask, aux_mask, density):
    mu, nu, p_total = three_centre.shape
    aux_pos, orb_pos, aux_count = lax.axis_index("aux"), lax.axis_index("orb"), lax.axis_size("aux")
    orbs = lax.axis_size("orb")
    pair = lax.dynamic_index_in_dim(pair_mask, orb_pos, 0, keepdims=False)
    aux = lax.dynamic_index_in_dim(aux_mask, aux_pos * (p_total // aux_count) // BLK, 1, keepdims=False)
    keep = jnp.concatenate([pair * aux, jnp.full((1,), aux_pos % 2, jnp.int32)])

    part = swap_bit(density.T, "orb", 1)
    sent = pack(three_centre, 0, mu // 64, 32, orbs)
    part, sent = lax.optimization_barrier((part, sent))
    columns = swap_bit(part, "orb", 2).reshape(orbs, density.shape[1], density.shape[0])
    sent = pack(three_centre, mu // 64, mu // 64, 32, orbs, sent)
    sent = append(sent, columns)
    sent, keep = lax.optimization_barrier((sent, keep))
    moved = lax.all_to_all(sent, "aux", split_axis=0, concat_axis=0, tiled=True)
    other = lax.ppermute(moved[:, mu // 2 :], "aux", [(i, i ^ 1) for i in range(aux_count)])
    return contract(moved, other, keep)


def solution(mesh):
    in_specs = (P("orb", "aux", None), P(), P(), P("orb", "aux"))
    out_specs = P("aux", "orb", None)
    return jax.shard_map(local, mesh=mesh, in_specs=in_specs, out_specs=out_specs, check_vma=False)
```

time: 196 us -> 152 us (0.78)
  waiting for transfers between devices: 126 us -> 1.9 us
  blocking collectives: 0 us -> 111 us
  starting transfers between devices: 37 us -> 4.91 us
  Pallas kernels: 15.3 us -> 27.1 us
  local copies, waits for them, and re-layouts: 15.7 us -> 4.49 us
    ppermute x7 -> x2, waiting for transfers between devices: 126 us -> 0.01 us  [swap_bit(): other = lax.ppermute(part, axis, [(i, i ^ bit) for i in range(count)])]
    all_to_all x0 -> x1, blocking collectives: none -> 111 us  [local(): moved = lax.all_to_all(sent, 'aux', split_axis=0, concat_axis=0, tiled=True)]
    ppermute x7 -> x2, starting transfers between devices: 27.4 us -> 4.83 us  [swap_bit(): other = lax.ppermute(part, axis, [(i, i ^ bit) for i in range(count)])]
    transpose x2 -> x0, local copies, waits for them, and re-layouts: 14.4 us -> none  [the longest x1 13.3 us: local(): jnp.transpose(three_centre, (2, 1, 0)).reshape(aux_count, p_local, nu, mu)]
    pallas_call x1 -> x4, Pallas kernels: 15.3 us -> 27.1 us  [the longest x1 17.1 us: contract(): pl.pallas_call(contract_kernel, out_shape=jax.ShapeDtypeStruct((HALF, 2 *...]
    all_to_all x1 -> x0, starting transfers between devices: 9.62 us -> none  [local(): moved = lax.all_to_all(sent, 'aux', split_axis=0, concat_axis=0, tiled=True)]
    unnamed x4 -> x8, local copies, waits for them, and re-layouts: 0.01 us -> 4.27 us
  transfers between devices with their start and end apart: 8 -> 3, of which waited for: 7 -> 1; matrix products, arithmetic and copies ran while one was open for 2% -> 1% of each run, Pallas kernels for 0% -> 6%
where the time goes in v2:
time: 152 us; the launch traced here: 151 us
  blocking collectives  111 us (73%)
  Pallas kernels  27.1 us (18%)
  starting transfers between devices  4.91 us (3%)
  local copies, waits for them, and re-layouts  4.49 us (3%)
  other arithmetic  1.98 us (1%)
  waiting for transfers between devices  1.9 us (1%)
    all_to_all x1, blocking collectives, local(): moved = lax.all_to_all(sent, 'aux', split_axis=0, concat_axis=0, tiled=True)  111 us
    pallas_call x1, Pallas kernels, contract(): pl.pallas_call(contract_kernel, out_shape=jax.ShapeDtypeStruct((HALF, 2 *...  17.1 us
    pallas_call x2, Pallas kernels, pack(): pl.pallas_call(pack_kernel, out_shape=jax.ShapeDtypeStruct((targets, mu /...  8.43 us
    ppermute x2, starting transfers between devices, swap_bit(): other = lax.ppermute(part, axis, [(i, i ^ bit) for i in range(count)])  4.83 us
    unnamed x8, local copies, waits for them, and re-layouts  4.27 us
  transfers between devices with their start and end apart: 3, of which 1 were waited for; matrix products, arithmetic and copies ran while one was open for 1% of the time, Pallas kernels for 6%

profile of v2, /device:TPU:1, one launch (start us, length us, event | category | flops | bytes accessed | tf_op | source)
XLA Modules:
  0.0 151.1 jit_solution(15833641958656746268)
XLA Ops:
  0.0 0.0 copy-start
  0.0 0.0 copy-start.3
  0.0 2.1 %collective-permute-start = (bf16[32,128]{1,0:T(8,128)(2,1)}, bf16[32,128]{1,0:T(8,128)(2,1)S(1)}, u32[]{:S(2)}, u32[]{:S(2)}) collective-permute-start(bf16[32,128]{1,0:T(8,128)(2,1)} %bitcast.16), channel_id=1, source_target_pairs={{0,1},{1,0},{2,3},{3,2},{4,5},{5,4},{6,7},{7,6},{8,9},{9,8},{10,11... | collective-permute-start | bytes 24584 | tf_op jit(solution)/shard_map/ppermute | solution.py:19
  2.1 0.0 copy-done
  2.1 0.2 dynamic-slice_reduce_fusion
  2.3 0.7 bitcast_multiply_fusion
  3.0 4.2 %shard_map.46.rest_0_ = bf16[32,68,16,128]{3,2,1,0:T(8,128)(2,1)} custom-call(bf16[128,16,2048]{2,1,0:T(8,128)(2,1)} %x_ref.3), custom_call_target="tpu_custom_call" | custom-call | bytes 8388608 | tf_op jit(solution)/shard_map/pallas_call | solution.py:42
  7.2 0.0 collective-permute-done
  7.2 0.0 copy-done.3
  7.2 2.7 %collective-permute-start.1 = (bf16[2,32,128]{2,1,0:T(8,128)(2,1)S(1)}, bf16[2,32,128]{2,1,0:T(8,128)(2,1)S(1)}, u32[]{:S(2)}, u32[]{:S(2)}) collective-permute-start(bf16[2,32,128]{2,1,0:T(8,128)(2,1)S(1)} %pad_maximum_fusion.1), channel_id=1, source_target_pairs={{0,2},{1,3},{2,0},{3,1},{4,6},{5,7},{6,4},{7,5},{8,10},{9,11},{10,... | collective-permute-start | bytes 49160 | tf_op jit(solution)/shard_map/ppermute | solution.py:19
  10.0 0.7 pad_add_fusion.keep_ref
  10.6 4.2 %shard_map.47.sent_ref = bf16[32,68,16,128]{3,2,1,0:T(8,128)(2,1)} custom-call(bf16[128,16,2048]{2,1,0:T(8,128)(2,1)} %x_ref.3, bf16[32,68,16,128]{3,2,1,0:T(8,128)(2,1)} %shard_map.46.rest_0_), custom_call_target="tpu_custom_call", output_to_operand_aliasing={{}: (1, {})} | custom-call | bytes 8388608 | tf_op jit(solution)/shard_map/pallas_call | solution.py:42
  14.8 0.0 collective-permute-done.1
  14.8 0.6 pad_maximum_fusion
  15.5 1.6 %shard_map.48 = bf16[32,68,16,128]{3,2,1,0:T(8,128)(2,1)} custom-call(bf16[4,32,128]{2,1,0:T(8,128)(2,1)} %bitcast.15, bf16[32,68,16,128]{3,2,1,0:T(8,128)(2,1)} %shard_map.47.sent_ref), custom_call_target="tpu_custom_call", output_to_operand_aliasing={{}: (1, {})} | custom-call | tf_op jit(solution)/shard_map/pallas_call | solution.py:66
  17.1 110.7 %all_to_all.5.x_ref.mine_ref = bf16[32,68,16,128]{3,2,1,0:T(8,128)(2,1)S(1)} all-to-all(bf16[32,68,16,128]{3,2,1,0:T(8,128)(2,1)} %shard_map.48), channel_id=1, replica_groups=mesh['aux'=32,'orb'=4] {'aux'}, dimensions={0} | all-to-all | bytes 17825792 | tf_op jit(solution)/shard_map/all_to_all | solution.py:148
  127.7 0.0 copy-start.1
  127.7 3.4 %copy-done.1 = bf16[32,68,16,128]{3,2,1,0:T(8,128)(2,1)} copy-done((bf16[32,68,16,128]{3,2,1,0:T(8,128)(2,1)}, bf16[32,68,16,128]{3,2,1,0:T(8,128)(2,1)S(1)}, u32[]{:S(2)}) %copy-start.1) | copy-done | bytes 8912920
  131.2 0.1 collective-permute-start.2
  131.3 1.9 %collective-permute-done.2.other_ref = bf16[32,4,16,128]{3,2,1,0:T(8,128)(2,1)S(1)} collective-permute-done((bf16[32,4,16,128]{3,2,1,0:T(8,128)(2,1)S(1)}, bf16[32,4,16,128]{3,2,1,0:T(8,128)(2,1)S(1)}, u32[]{:S(2)}, u32[]{:S(2)}) %collective-permute-start.2) | collective-permute-done | bytes 524320 | tf_op jit(solution)/shard_map/ppermute | solution.py:149
  133.2 0.0 copy-start.2
  133.2 0.8 copy-done.2
  134.0 17.1 %shard_map.49 = bf16[64,128,1024]{2,1,0:T(8,128)(2,1)} custom-call(s32[5]{0:T(128)} %pad_add_fusion.keep_ref, bf16[32,68,16,128]{3,2,1,0:T(8,128)(2,1)} %copy-done.1, bf16[32,68,16,128]{3,2,1,0:T(8,128)(2,1)} %copy-done.1, bf16[32,4,16,128]{3,2,1,0:T(8,128)(2,1)} %copy-done.2), custom_call_target="tpu_custom_call" | custom-call | flops 8589934592 | bytes 27262976 | tf_op jit(solution)/shard_map/pallas_call | solution.py:111
  (4 shorter events, 0.1 us)
Async XLA Ops:
  0.0 2.1 %copy-start = (s32[4,16]{1,0:T(4,128)S(1)}, s32[4,16]{1,0:T(4,128)}, u32[]{:S(2)}) copy-start(s32[4,16]{1,0:T(4,128)} %param.6) | copy-start | bytes 772
  0.0 7.2 %copy-start.3 = (bf16[128,32]{0,1:T(8,128)(2,1)S(1)}, bf16[128,32]{0,1:T(8,128)(2,1)}, u32[]{:S(2)}) copy-start(bf16[128,32]{0,1:T(8,128)(2,1)} %param.7) | copy-start | bytes 24580
  0.0 7.2 %collective-permute-start = (bf16[32,128]{1,0:T(8,128)(2,1)}, bf16[32,128]{1,0:T(8,128)(2,1)S(1)}, u32[]{:S(2)}, u32[]{:S(2)}) collective-permute-start(bf16[32,128]{1,0:T(8,128)(2,1)} %bitcast.16), channel_id=1, source_target_pairs={{0,1},{1,0},{2,3},{3,2},{4,5},{5,4},{6,7},{7,6},{8,9},{9,8},{10,11... | collective-permute-start | bytes 24584 | tf_op jit(solution)/shard_map/ppermute | solution.py:19
  7.2 7.6 %collective-permute-start.1 = (bf16[2,32,128]{2,1,0:T(8,128)(2,1)S(1)}, bf16[2,32,128]{2,1,0:T(8,128)(2,1)S(1)}, u32[]{:S(2)}, u32[]{:S(2)}) collective-permute-start(bf16[2,32,128]{2,1,0:T(8,128)(2,1)S(1)} %pad_maximum_fusion.1), channel_id=1, source_target_pairs={{0,2},{1,3},{2,0},{3,1},{4,6},{5,7},{6,4},{7,5},{8,10},{9,11},{10,... | collective-permute-start | bytes 49160 | tf_op jit(solution)/shard_map/ppermute | solution.py:19
  127.7 3.4 %copy-start.1 = (bf16[32,68,16,128]{3,2,1,0:T(8,128)(2,1)}, bf16[32,68,16,128]{3,2,1,0:T(8,128)(2,1)S(1)}, u32[]{:S(2)}) copy-start(bf16[32,68,16,128]{3,2,1,0:T(8,128)(2,1)S(1)} %all_to_all.5.x_ref.mine_ref) | copy-start | bytes 26738692
  131.2 2.0 %collective-permute-start.2 = (bf16[32,4,16,128]{3,2,1,0:T(8,128)(2,1)S(1)}, bf16[32,4,16,128]{3,2,1,0:T(8,128)(2,1)S(1)}, u32[]{:S(2)}, u32[]{:S(2)}) collective-permute-start(bf16[32,4,16,128]{3,2,1,0:T(8,128)(2,1)S(1)} %slice.4), channel_id=1, source_target_pairs={{0,4},{4,0},{8,12},{12,8},{16,20},{20,16},{24,28},{28,24},{32,36},... | collective-permute-start | bytes 1572872 | tf_op jit(solution)/shard_map/ppermute | solution.py:149
  133.2 0.8 copy-start.2

commit v3 on v2

v3 whole, which is shorter than its diff:
```python
import jax
import jax.numpy as jnp
from jax import lax
from jax.experimental import pallas as pl
from jax.experimental.pallas import tpu as pltpu
from jax.sharding import PartitionSpec as P

BLK = 128
LANES = 128
HALF = 64
GROUP = 16
PAIRS = 8
SUBS = 2
PITCH = 24
VMEM = 60 << 20


def pack_kernel(x_ref, *rest):
    o_ref = rest[-1]
    for group in range(x_ref.shape[0] // GROUP):
        top = group * GROUP
        for block in range(x_ref.shape[2] // LANES):
            lanes = slice(block * LANES, (block + 1) * LANES)
            low, high = x_ref[top : top + PAIRS, :, lanes], x_ref[top + PAIRS : top + GROUP, :, lanes]
            rows = slice(group * PAIRS, (group + 1) * PAIRS)
            o_ref[2 * block, rows] = jnp.concatenate([low[..., :HALF], high[..., :HALF]], axis=-1)
            o_ref[2 * block + 1, rows] = jnp.concatenate([low[..., HALF:], high[..., HALF:]], axis=-1)


def pack(three_centre, first, count, rows, extra, earlier=None):
    mu, nu, p_total = three_centre.shape
    targets = p_total // HALF
    args, specs, aliases = [three_centre], [pl.BlockSpec((rows, nu, p_total), lambda i: (first + i, 0, 0))], {}
    if earlier is not None:
        args, specs, aliases = args + [earlier], specs + [pl.BlockSpec(memory_space=pl.ANY)], {1: 0}
    return pl.pallas_call(
        pack_kernel,
        out_shape=jax.ShapeDtypeStruct((targets, mu // 2 + extra, nu, LANES), jnp.bfloat16),
        grid=(count,),
        in_specs=specs,
        out_specs=pl.BlockSpec((targets, rows // 2, nu, LANES), lambda i: (0, first + i, 0, 0)),
        input_output_aliases=aliases,
        compiler_params=pltpu.CompilerParams(vmem_limit_bytes=VMEM),
        cost_estimate=pl.CostEstimate(
            flops=0, bytes_accessed=4 * count * rows * nu * p_total, transcendentals=0
        ),
    )(*args)


def append_kernel(*refs):
    o_ref, parts = refs[-1], refs[:-2]
    half = parts[0].shape[0] // 2
    for step, part in zip((0, -1, 1, 2), parts):
        orb = lax.rem(lax.axis_index("orb") + len(parts) + step, len(parts))
        for target in range(o_ref.shape[0]):
            core = target % 2
            o_ref[target, orb] = part[core * half : (core + 1) * half, :]


def append(sent, parts):
    targets, rows, nu, lanes = sent.shape
    orbs = len(parts)
    return pl.pallas_call(
        append_kernel,
        out_shape=jax.ShapeDtypeStruct(sent.shape, sent.dtype),
        grid=(1,),
        in_specs=[pl.BlockSpec(part.shape, lambda i: (0, 0)) for part in parts]
        + [pl.BlockSpec(memory_space=pl.ANY)],
        out_specs=pl.BlockSpec((targets, orbs, nu, lanes), lambda i: (0, rows // orbs - 1, 0, 0)),
        input_output_aliases={orbs: 0},
        compiler_params=pltpu.CompilerParams(vmem_limit_bytes=50 << 20),
    )(*parts, sent)


def contract_kernel(pair_ref, aux_ref, x_ref, mine_ref, other_ref, o_ref, dens_ref, rows_ref):
    sources, _, nu, _ = x_ref.shape
    depth = sources * nu
    _, orbs, half, lanes = mine_ref.shape
    aux_pos, orb_pos = lax.axis_index("aux"), lax.axis_index("orb")

    @pl.when(pl.program_id(0) == 0)
    def _():
        upper = lax.rem(aux_pos, 2) == 1
        column = lax.div(aux_pos * HALF, BLK)
        for orb in range(orbs):
            keep = (pair_ref[orb_pos, orb] * aux_ref[orb, column]).astype(jnp.float32).astype(jnp.bfloat16)
            mine, other = mine_ref[:, orb], other_ref[:, orb]
            low, high = jnp.where(upper, other, mine), jnp.where(upper, mine, other)
            whole = jnp.stack([low, high], axis=1).reshape(sources * 2 * half, lanes)
            dens_ref[orb * lanes : (orb + 1) * lanes, :] = whole.T * keep

    def order_rows(sub, pair):
        turned = x_ref[:, sub * PAIRS + pair].reshape(depth, LANES).T.astype(jnp.float32)
        for k in range(depth // LANES):
            piece = turned[:, k * LANES : (k + 1) * LANES]
            base = k * HALF * PITCH + pair
            rows_ref[sub, pl.ds(base, HALF, stride=PITCH), :] = piece[:HALF]
            rows_ref[sub, pl.ds(base + PAIRS, HALF, stride=PITCH), :] = piece[HALF:]

    def multiply(sub):
        pieces = []
        for k in range(depth // LANES):
            piece = rows_ref[sub, k * HALF * PITCH : (k + 1) * HALF * PITCH, :].reshape(HALF, PITCH, LANES)
            pieces.append(piece[:, :GROUP].reshape(HALF * GROUP, LANES).astype(jnp.bfloat16))
        product = jnp.dot(jnp.concatenate(pieces, axis=1), dens_ref[...], preferred_element_type=jnp.float32)
        mus = slice(sub * GROUP, (sub + 1) * GROUP)
        o_ref[:, mus] = product.astype(jnp.bfloat16).reshape(HALF, GROUP, -1)

    for sub in range(SUBS):
        for pair in range(PAIRS):
            order_rows(sub, pair)
    for sub in range(SUBS):
        multiply(sub)


def contract(moved, other, pair_mask, aux_mask):
    sources, orbs, nu, _ = other.shape
    pairs = moved.shape[1] - orbs
    sig = sources * 2 * nu
    return pl.pallas_call(
        contract_kernel,
        out_shape=jax.ShapeDtypeStruct((HALF, 2 * pairs, sig), jnp.bfloat16),
        grid=(pairs // (SUBS * PAIRS),),
        in_specs=[
            pl.BlockSpec(memory_space=pltpu.SMEM),
            pl.BlockSpec(memory_space=pltpu.SMEM),
            pl.BlockSpec((sources, SUBS * PAIRS, nu, LANES), lambda i: (0, i, 0, 0)),
            pl.BlockSpec((sources, orbs, nu, LANES), lambda i: (0, pairs // orbs, 0, 0)),
            pl.BlockSpec(other.shape, lambda i: (0, 0, 0, 0)),
        ],
        out_specs=pl.BlockSpec((HALF, SUBS * GROUP, sig), lambda i: (0, i, 0)),
        scratch_shapes=[
            pltpu.VMEM((orbs * LANES, sig), jnp.bfloat16),
            pltpu.VMEM((SUBS, orbs * HALF * PITCH, LANES), jnp.float32),
        ],
        compiler_params=pltpu.CompilerParams(vmem_limit_bytes=36 << 20),
        cost_estimate=pl.CostEstimate(
            flops=4 * HALF * pairs * orbs * LANES * sig, bytes_accessed=26 << 20, transcendentals=0
        ),
    )(pair_mask, aux_mask, moved, moved, other)


def local(three_centre, pair_mask, aux_mask, density):
    mu, nu, p_total = three_centre.shape
    aux_count, orbs = lax.axis_size("aux"), lax.axis_size("orb")
    own = density.T
    up, down = [(i, (i + 1) % orbs) for i in range(orbs)], [(i, (i - 1) % orbs) for i in range(orbs)]
    before = lax.ppermute(own, "orb", up)
    after = lax.ppermute(own, "orb", down)
    sent = pack(three_centre, 0, mu // 64, 32, orbs)
    before, after, sent = lax.optimization_barrier((before, after, sent))
    across = lax.ppermute(before, "orb", up)
    sent = pack(three_centre, mu // 64, mu // 64, 32, orbs, sent)
    sent = append(sent, (own, before, after, across))
    moved = lax.all_to_all(sent, "aux", split_axis=0, concat_axis=0, tiled=True)
    other = lax.ppermute(moved[:, mu // 2 :], "aux", [(i, i ^ 1) for i in range(aux_count)])
    return contract(moved, other, pair_mask, aux_mask)


def solution(mesh):
    in_specs = (P("orb", "aux", None), P(), P(), P("orb", "aux"))
    out_specs = P("aux", "orb", None)
    return jax.shard_map(local, mesh=mesh, in_specs=in_specs, out_specs=out_specs, check_vma=False)
```

time: 152 us -> 142 us (0.934)
  local copies, waits for them, and re-layouts: 4.49 us -> 0.05 us
  Pallas kernels: 27.1 us -> 24.4 us
  other arithmetic: 1.98 us -> 0 us
    unnamed x8 -> x6, local copies, waits for them, and re-layouts: 4.27 us -> 0.01 us
    pallas_call x1, Pallas kernels: 17.1 us -> 15.1 us  [contract(): pl.pallas_call(contract_kernel, out_shape=jax.ShapeDtypeStruct((HALF, 2 *...]
    ppermute x2 -> x3, starting transfers between devices: 4.83 us -> 3.66 us  [the longest x1 3.56 us: local(): after = lax.ppermute(own, 'orb', down)]
  transfers between devices with their start and end apart: 3 -> 4, of which waited for: 1 -> 1; matrix products, arithmetic and copies ran while one was open for 1% -> 0% of each run, Pallas kernels for 6% -> 6%
where the time goes in v3:
time: 142 us
  blocking collectives  112 us (79%)
  Pallas kernels  24.4 us (17%)
  starting transfers between devices  3.75 us (3%)
  waiting for transfers between devices  1.9 us (1%)
    all_to_all x1, blocking collectives, local(): moved = lax.all_to_all(sent, 'aux', split_axis=0, concat_axis=0, tiled=True)  112 us
    pallas_call x1, Pallas kernels, contract(): pl.pallas_call(contract_kernel, out_shape=jax.ShapeDtypeStruct((HALF, 2 *...  15.1 us
    pallas_call x2, Pallas kernels, pack(): pl.pallas_call(pack_kernel, out_shape=jax.ShapeDtypeStruct((targets, mu /...  8.43 us
    ppermute x1, starting transfers between devices, local(): after = lax.ppermute(own, 'orb', down)  3.56 us
  transfers between devices with their start and end apart: 4, of which 1 were waited for; matrix products, arithmetic and copies ran while one was open for 0% of the time, Pallas kernels for 6%

profile of v3, /device:TPU:1, one launch (start us, length us, event | category | flops | bytes accessed | tf_op | source)
XLA Modules:
  0.0 142.0 jit_solution(11979606953559596693)
XLA Ops:
  0.0 3.6 %collective-permute-start.1 = (bf16[32,128]{1,0:T(8,128)(2,1)}, bf16[32,128]{1,0:T(8,128)(2,1)S(1)}, u32[]{:S(2)}, u32[]{:S(2)}) collective-permute-start(bf16[32,128]{1,0:T(8,128)(2,1)} %bitcast.1), channel_id=1, source_target_pairs={{0,3},{1,0},{2,1},{3,2},{4,7},{5,4},{6,5},{7,6},{8,11},{9,8},{10,9... | collective-permute-start | bytes 24584 | tf_op jit(solution)/shard_map/ppermute | solution.py:149
  3.6 0.0 collective-permute-start
  3.6 4.2 %shard_map.46.rest_0_ = bf16[32,68,16,128]{3,2,1,0:T(8,128)(2,1)} custom-call(bf16[128,16,2048]{2,1,0:T(8,128)(2,1)} %x_ref.3), custom_call_target="tpu_custom_call" | custom-call | bytes 8388608 | tf_op jit(solution)/shard_map/pallas_call | solution.py:36
  7.8 0.0 copy-start
  7.8 0.0 collective-permute-done.1.refs_2_
  7.8 0.0 collective-permute-done.refs_1_
  7.8 0.1 collective-permute-start.2
  7.9 4.2 %shard_map.47.refs_4_ = bf16[32,68,16,128]{3,2,1,0:T(8,128)(2,1)} custom-call(bf16[128,16,2048]{2,1,0:T(8,128)(2,1)} %x_ref.3, bf16[32,68,16,128]{3,2,1,0:T(8,128)(2,1)} %shard_map.46.rest_0_), custom_call_target="tpu_custom_call", output_to_operand_aliasing={{}: (1, {})} | custom-call | bytes 8388608 | tf_op jit(solution)/shard_map/pallas_call | solution.py:36
  12.1 0.0 collective-permute-done.2.refs_3_
  12.1 0.0 copy-done
  12.1 0.9 shard_map.48
  13.0 0.0 copy-start.1
  13.0 0.0 copy-start.2
  13.0 111.9 %all_to_all.5.x_ref.mine_ref = bf16[32,68,16,128]{3,2,1,0:T(8,128)(2,1)S(1)} all-to-all(bf16[32,68,16,128]{3,2,1,0:T(8,128)(2,1)} %shard_map.48), channel_id=1, replica_groups=mesh['aux'=32,'orb'=4] {'aux'}, dimensions={0} | all-to-all | bytes 17825792 | tf_op jit(solution)/shard_map/all_to_all | solution.py:155
  124.9 0.1 collective-permute-start.3
  125.0 1.9 %collective-permute-done.3.other_ref = bf16[32,4,16,128]{3,2,1,0:T(8,128)(2,1)S(1)} collective-permute-done((bf16[32,4,16,128]{3,2,1,0:T(8,128)(2,1)S(1)}, bf16[32,4,16,128]{3,2,1,0:T(8,128)(2,1)S(1)}, u32[]{:S(2)}, u32[]{:S(2)}) %collective-permute-start.3) | collective-permute-done | bytes 524320 | tf_op jit(solution)/shard_map/ppermute | solution.py:156
  126.9 0.0 copy-done.1
  126.9 0.0 copy-done.2
  126.9 15.1 %shard_map.49 = bf16[64,128,1024]{2,1,0:T(8,128)(2,1)} custom-call(s32[4,4]{1,0:T(4,128)S(1)} %copy-done.1, s32[4,16]{1,0:T(4,128)S(1)} %copy-done.2, bf16[32,68,16,128]{3,2,1,0:T(8,128)(2,1)S(1)} %all_to_all.5.x_ref.mine_ref, bf16[32,68,16,128]{3,2,1,0:T(8,128)(2,1)S(1)} %all_to_all.5.x_ref.mine_ref, ...), custom_call_target="tpu_custom_call" | custom-call | flops 8589934592 | bytes 27262976 | tf_op jit(solution)/shard_map/pallas_call | solution.py:120
  (1 shorter events, 0.0 us)
Async XLA Ops:
  0.0 7.8 %collective-permute-start.1 = (bf16[32,128]{1,0:T(8,128)(2,1)}, bf16[32,128]{1,0:T(8,128)(2,1)S(1)}, u32[]{:S(2)}, u32[]{:S(2)}) collective-permute-start(bf16[32,128]{1,0:T(8,128)(2,1)} %bitcast.1), channel_id=1, source_target_pairs={{0,3},{1,0},{2,1},{3,2},{4,7},{5,4},{6,5},{7,6},{8,11},{9,8},{10,9... | collective-permute-start | bytes 24584 | tf_op jit(solution)/shard_map/ppermute | solution.py:149
  3.6 4.2 %collective-permute-start = (bf16[32,128]{1,0:T(8,128)(2,1)}, bf16[32,128]{1,0:T(8,128)(2,1)S(1)}, u32[]{:S(2)}, u32[]{:S(2)}) collective-permute-start(bf16[32,128]{1,0:T(8,128)(2,1)} %bitcast.2), channel_id=1, source_target_pairs={{0,1},{1,2},{2,3},{3,0},{4,5},{5,6},{6,7},{7,4},{8,9},{9,10},{10,1... | collective-permute-start | bytes 24584 | tf_op jit(solution)/shard_map/ppermute | solution.py:148
  7.8 4.3 %copy-start = (bf16[128,32]{0,1:T(8,128)(2,1)S(1)}, bf16[128,32]{0,1:T(8,128)(2,1)}, u32[]{:S(2)}) copy-start(bf16[128,32]{0,1:T(8,128)(2,1)} %param.7) | copy-start | bytes 24580
  7.8 4.3 %collective-permute-start.2 = (bf16[32,128]{1,0:T(8,128)(2,1)S(1)}, bf16[32,128]{1,0:T(8,128)(2,1)S(1)}, u32[]{:S(2)}, u32[]{:S(2)}) collective-permute-start(bf16[32,128]{1,0:T(8,128)(2,1)S(1)} %collective-permute-done.refs_1_), channel_id=1, source_target_pairs={{0,1},{1,2},{2,3},{3,0},{4,5},{5,6},{6,7},{7,4},{8,9},{9,10},{10,1... | collective-permute-start | bytes 24584 | tf_op jit(solution)/shard_map/ppermute | solution.py:152
  13.0 113.9 %copy-start.1 = (s32[4,4]{1,0:T(4,128)S(1)}, s32[4,4]{1,0:T(4,128)}, u32[]{:S(2)}) copy-start(s32[4,4]{1,0:T(4,128)} %pair_ref.1) | copy-start | bytes 196
  13.0 113.9 %copy-start.2 = (s32[4,16]{1,0:T(4,128)S(1)}, s32[4,16]{1,0:T(4,128)}, u32[]{:S(2)}) copy-start(s32[4,16]{1,0:T(4,128)} %aux_ref.1) | copy-start | bytes 772
  124.9 2.0 %collective-permute-start.3 = (bf16[32,4,16,128]{3,2,1,0:T(8,128)(2,1)S(1)}, bf16[32,4,16,128]{3,2,1,0:T(8,128)(2,1)S(1)}, u32[]{:S(2)}, u32[]{:S(2)}) collective-permute-start(bf16[32,4,16,128]{3,2,1,0:T(8,128)(2,1)S(1)} %slice.4), channel_id=1, source_target_pairs={{0,4},{4,0},{8,12},{12,8},{16,20},{20,16},{24,28},{28,24},{32,36},... | collective-permute-start | bytes 1572872 | tf_op jit(solution)/shard_map/ppermute | solution.py:156

commit v4 on v3

--- a/solution.py
+++ b/solution.py
@@ -30,7 +30,7 @@
 def pack(three_centre, first, count, rows, extra, earlier=None):
     mu, nu, p_total = three_centre.shape
     targets = p_total // HALF
-    args, specs, aliases = [three_centre], [pl.BlockSpec((rows, nu, p_total), lambda i: (first + i, 0, 0))], {}
+    args, specs, aliases = [pltpu.with_memory_space_constraint(three_centre, pltpu.HBM)], [pl.BlockSpec((rows, nu, p_total), lambda i: (first + i, 0, 0))], {}
     if earlier is not None:
         args, specs, aliases = args + [earlier], specs + [pl.BlockSpec(memory_space=pl.ANY)], {1: 0}
     return pl.pallas_call(
@@ -40,7 +40,7 @@
         in_specs=specs,
         out_specs=pl.BlockSpec((targets, rows // 2, nu, LANES), lambda i: (0, first + i, 0, 0)),
         input_output_aliases=aliases,
-        compiler_params=pltpu.CompilerParams(vmem_limit_bytes=VMEM),
+        compiler_params=pltpu.CompilerParams(vmem_limit_bytes=28 << 20),
         cost_estimate=pl.CostEstimate(
             flops=0, bytes_accessed=4 * count * rows * nu * p_total, transcendentals=0
         ),
@@ -68,7 +68,7 @@
         + [pl.BlockSpec(memory_space=pl.ANY)],
         out_specs=pl.BlockSpec((targets, orbs, nu, lanes), lambda i: (0, rows // orbs - 1, 0, 0)),
         input_output_aliases={orbs: 0},
-        compiler_params=pltpu.CompilerParams(vmem_limit_bytes=50 << 20),
+        compiler_params=pltpu.CompilerParams(vmem_limit_bytes=28 << 20),
     )(*parts, sent)
 
 
@@ -145,12 +145,9 @@
     aux_count, orbs = lax.axis_size("aux"), lax.axis_size("orb")
     own = density.T
     up, down = [(i, (i + 1) % orbs) for i in range(orbs)], [(i, (i - 1) % orbs) for i in range(orbs)]
-    before = lax.ppermute(own, "orb", up)
-    after = lax.ppermute(own, "orb", down)
-    sent = pack(three_centre, 0, mu // 64, 32, orbs)
-    before, after, sent = lax.optimization_barrier((before, after, sent))
-    across = lax.ppermute(before, "orb", up)
-    sent = pack(three_centre, mu // 64, mu // 64, 32, orbs, sent)
+    two_up = [(i, (i + 2) % orbs) for i in range(orbs)]
+    before, after, across = (lax.ppermute(own, "orb", pairs) for pairs in (up, down, two_up))
+    sent = pack(three_centre, 0, mu // 32, 32, orbs)
     sent = append(sent, (own, before, after, across))
     moved = lax.all_to_all(sent, "aux", split_axis=0, concat_axis=0, tiled=True)
     other = lax.ppermute(moved[:, mu // 2 :], "aux", [(i, i ^ 1) for i in range(aux_count)])

time: 142 us -> 140 us (0.986)
  Pallas kernels: 24.4 us -> 21.6 us
  starting transfers between devices: 3.75 us -> 5.29 us
    pallas_call x2 -> x1, Pallas kernels: 8.43 us -> 6.45 us  [pack(): pl.pallas_call(pack_kernel, out_shape=jax.ShapeDtypeStruct((targets, mu /...]
    ppermute x3, starting transfers between devices: 3.66 us -> 5.21 us  [local(): lax.ppermute(own, 'orb', pairs)]
  transfers between devices with their start and end apart: 4 -> 4, of which waited for: 1 -> 1; matrix products, arithmetic and copies ran while one was open for 0% -> 0% of each run, Pallas kernels for 6% -> 5%
where the time goes in v4:
time: 140 us
  blocking collectives  111 us (79%)
  Pallas kernels  21.6 us (15%)
  starting transfers between devices  5.29 us (4%)
  waiting for transfers between devices  1.9 us (1%)
    all_to_all x1, blocking collectives, local(): moved = lax.all_to_all(sent, 'aux', split_axis=0, concat_axis=0, tiled=True)  111 us
    pallas_call x1, Pallas kernels, contract(): pl.pallas_call(contract_kernel, out_shape=jax.ShapeDtypeStruct((HALF, 2 *...  15.1 us
    pallas_call x1, Pallas kernels, pack(): pl.pallas_call(pack_kernel, out_shape=jax.ShapeDtypeStruct((targets, mu /...  6.45 us
    ppermute x3, starting transfers between devices, local(): lax.ppermute(own, 'orb', pairs)  5.21 us
  transfers between devices with their start and end apart: 4, of which 1 were waited for; matrix products, arithmetic and copies ran while one was open for 0% of the time, Pallas kernels for 5%

profile of v4, /device:TPU:1, one launch (start us, length us, event | category | flops | bytes accessed | tf_op | source)
XLA Modules:
  0.0 139.7 jit_solution(9634942256953535039)
XLA Ops:
  0.0 0.0 copy-start
  0.0 3.7 %collective-permute-start.2 = (bf16[32,128]{1,0:T(8,128)(2,1)}, bf16[32,128]{1,0:T(8,128)(2,1)S(1)}, u32[]{:S(2)}, u32[]{:S(2)}) collective-permute-start(bf16[32,128]{1,0:T(8,128)(2,1)} %bitcast.1), channel_id=1, source_target_pairs={{0,2},{1,3},{2,0},{3,1},{4,6},{5,7},{6,4},{7,5},{8,10},{9,11},{10,... | collective-permute-start | bytes 24584 | tf_op jit(solution)/shard_map/ppermute | solution.py:149
  3.7 0.8 collective-permute-start.1
  4.5 0.7 collective-permute-start
  5.2 6.5 %shard_map.46.refs_4_ = bf16[32,68,16,128]{3,2,1,0:T(8,128)(2,1)S(1)} custom-call(bf16[128,16,2048]{2,1,0:T(8,128)(2,1)} %x_ref.1), custom_call_target="tpu_custom_call" | custom-call | bytes 16777216 | tf_op jit(solution)/shard_map/pallas_call | solution.py:36
  11.7 0.0 collective-permute-done.2.refs_3_
  11.7 0.0 collective-permute-done.1.refs_2_
  11.7 0.0 collective-permute-done.refs_1_
  11.7 0.0 copy-done
  11.7 0.1 shard_map.47
  11.9 0.0 copy-start.1
  11.9 0.0 copy-start.2
  11.9 110.7 %all_to_all.5.x_ref.mine_ref = bf16[32,68,16,128]{3,2,1,0:T(8,128)(2,1)S(1)} all-to-all(bf16[32,68,16,128]{3,2,1,0:T(8,128)(2,1)S(1)} %shard_map.47), channel_id=1, replica_groups=mesh['aux'=32,'orb'=4] {'aux'}, dimensions={0} | all-to-all | bytes 17825792 | tf_op jit(solution)/shard_map/all_to_all | solution.py:152
  122.7 0.1 collective-permute-start.3
  122.8 1.9 %collective-permute-done.3.other_ref = bf16[32,4,16,128]{3,2,1,0:T(8,128)(2,1)S(1)} collective-permute-done((bf16[32,4,16,128]{3,2,1,0:T(8,128)(2,1)S(1)}, bf16[32,4,16,128]{3,2,1,0:T(8,128)(2,1)S(1)}, u32[]{:S(2)}, u32[]{:S(2)}) %collective-permute-start.3) | collective-permute-done | bytes 524320 | tf_op jit(solution)/shard_map/ppermute | solution.py:153
  124.7 0.0 copy-done.1
  124.7 0.0 copy-done.2
  124.7 15.1 %shard_map.48 = bf16[64,128,1024]{2,1,0:T(8,128)(2,1)} custom-call(s32[4,4]{1,0:T(4,128)S(1)} %copy-done.1, s32[4,16]{1,0:T(4,128)S(1)} %copy-done.2, bf16[32,68,16,128]{3,2,1,0:T(8,128)(2,1)S(1)} %all_to_all.5.x_ref.mine_ref, bf16[32,68,16,128]{3,2,1,0:T(8,128)(2,1)S(1)} %all_to_all.5.x_ref.mine_ref, ...), custom_call_target="tpu_custom_call" | custom-call | flops 8589934592 | bytes 27262976 | tf_op jit(solution)/shard_map/pallas_call | solution.py:120
  (1 shorter events, 0.0 us)
Async XLA Ops:
  0.0 11.7 %copy-start = (bf16[128,32]{0,1:T(8,128)(2,1)S(1)}, bf16[128,32]{0,1:T(8,128)(2,1)}, u32[]{:S(2)}) copy-start(bf16[128,32]{0,1:T(8,128)(2,1)} %param.7) | copy-start | bytes 24580
  0.0 11.7 %collective-permute-start.2 = (bf16[32,128]{1,0:T(8,128)(2,1)}, bf16[32,128]{1,0:T(8,128)(2,1)S(1)}, u32[]{:S(2)}, u32[]{:S(2)}) collective-permute-start(bf16[32,128]{1,0:T(8,128)(2,1)} %bitcast.1), channel_id=1, source_target_pairs={{0,2},{1,3},{2,0},{3,1},{4,6},{5,7},{6,4},{7,5},{8,10},{9,11},{10,... | collective-permute-start | bytes 24584 | tf_op jit(solution)/shard_map/ppermute | solution.py:149
  3.7 7.9 %collective-permute-start.1 = (bf16[32,128]{1,0:T(8,128)(2,1)}, bf16[32,128]{1,0:T(8,128)(2,1)S(1)}, u32[]{:S(2)}, u32[]{:S(2)}) collective-permute-start(bf16[32,128]{1,0:T(8,128)(2,1)} %bitcast.2), channel_id=1, source_target_pairs={{0,3},{1,0},{2,1},{3,2},{4,7},{5,4},{6,5},{7,6},{8,11},{9,8},{10,9... | collective-permute-start | bytes 24584 | tf_op jit(solution)/shard_map/ppermute | solution.py:149
  4.5 7.2 %collective-permute-start = (bf16[32,128]{1,0:T(8,128)(2,1)}, bf16[32,128]{1,0:T(8,128)(2,1)S(1)}, u32[]{:S(2)}, u32[]{:S(2)}) collective-permute-start(bf16[32,128]{1,0:T(8,128)(2,1)} %bitcast.3), channel_id=1, source_target_pairs={{0,1},{1,2},{2,3},{3,0},{4,5},{5,6},{6,7},{7,4},{8,9},{9,10},{10,1... | collective-permute-start | bytes 24584 | tf_op jit(solution)/shard_map/ppermute | solution.py:149
  11.9 112.8 %copy-start.1 = (s32[4,4]{1,0:T(4,128)S(1)}, s32[4,4]{1,0:T(4,128)}, u32[]{:S(2)}) copy-start(s32[4,4]{1,0:T(4,128)} %pair_ref.1) | copy-start | bytes 196
  11.9 112.8 %copy-start.2 = (s32[4,16]{1,0:T(4,128)S(1)}, s32[4,16]{1,0:T(4,128)}, u32[]{:S(2)}) copy-start(s32[4,16]{1,0:T(4,128)} %aux_ref.1) | copy-start | bytes 772
  122.7 2.0 %collective-permute-start.3 = (bf16[32,4,16,128]{3,2,1,0:T(8,128)(2,1)S(1)}, bf16[32,4,16,128]{3,2,1,0:T(8,128)(2,1)S(1)}, u32[]{:S(2)}, u32[]{:S(2)}) collective-permute-start(bf16[32,4,16,128]{3,2,1,0:T(8,128)(2,1)S(1)} %slice.4), channel_id=1, source_target_pairs={{0,4},{4,0},{8,12},{12,8},{16,20},{20,16},{24,28},{28,24},{32,36},... | collective-permute-start | bytes 1572872 | tf_op jit(solution)/shard_map/ppermute | solution.py:153

commit v5 on v4

--- a/solution.py
+++ b/solution.py
@@ -40,7 +40,7 @@
         in_specs=specs,
         out_specs=pl.BlockSpec((targets, rows // 2, nu, LANES), lambda i: (0, first + i, 0, 0)),
         input_output_aliases=aliases,
-        compiler_params=pltpu.CompilerParams(vmem_limit_bytes=28 << 20),
+        compiler_params=pltpu.CompilerParams(vmem_limit_bytes=36 << 20),
         cost_estimate=pl.CostEstimate(
             flops=0, bytes_accessed=4 * count * rows * nu * p_total, transcendentals=0
         ),
@@ -50,8 +50,8 @@
 def append_kernel(*refs):
     o_ref, parts = refs[-1], refs[:-2]
     half = parts[0].shape[0] // 2
-    for step, part in zip((0, -1, 1, 2), parts):
-        orb = lax.rem(lax.axis_index("orb") + len(parts) + step, len(parts))
+    for step, part in enumerate(parts):
+        orb = lax.axis_index("orb") ^ step
         for target in range(o_ref.shape[0]):
             core = target % 2
             o_ref[target, orb] = part[core * half : (core + 1) * half, :]
@@ -68,7 +68,7 @@
         + [pl.BlockSpec(memory_space=pl.ANY)],
         out_specs=pl.BlockSpec((targets, orbs, nu, lanes), lambda i: (0, rows // orbs - 1, 0, 0)),
         input_output_aliases={orbs: 0},
-        compiler_params=pltpu.CompilerParams(vmem_limit_bytes=28 << 20),
+        compiler_params=pltpu.CompilerParams(vmem_limit_bytes=36 << 20),
     )(*parts, sent)
 
 
@@ -144,11 +144,9 @@
     mu, nu, p_total = three_centre.shape
     aux_count, orbs = lax.axis_size("aux"), lax.axis_size("orb")
     own = density.T
-    up, down = [(i, (i + 1) % orbs) for i in range(orbs)], [(i, (i - 1) % orbs) for i in range(orbs)]
-    two_up = [(i, (i + 2) % orbs) for i in range(orbs)]
-    before, after, across = (lax.ppermute(own, "orb", pairs) for pairs in (up, down, two_up))
-    sent = pack(three_centre, 0, mu // 32, 32, orbs)
-    sent = append(sent, (own, before, after, across))
+    others = [lax.ppermute(own, "orb", [(i, i ^ step) for i in range(orbs)]) for step in range(1, orbs)]
+    sent = pack(three_centre, 0, mu // 64, 64, orbs)
+    sent = append(sent, (own, *others))
     moved = lax.all_to_all(sent, "aux", split_axis=0, concat_axis=0, tiled=True)
     other = lax.ppermute(moved[:, mu // 2 :], "aux", [(i, i ^ 1) for i in range(aux_count)])
     return contract(moved, other, pair_mask, aux_mask)

time: 140 us -> 138 us (0.986)
  transfers between devices with their start and end apart: 4 -> 4, of which waited for: 1 -> 1; matrix products, arithmetic and copies ran while one was open for 0% -> 0% of each run, Pallas kernels for 5% -> 4%
where the time goes in v5:
time: 138 us
  blocking collectives  111 us (80%)
  Pallas kernels  21.4 us (16%)
  starting transfers between devices  4.3 us (3%)
  waiting for transfers between devices  1.9 us (1%)
    all_to_all x1, blocking collectives, local(): moved = lax.all_to_all(sent, 'aux', split_axis=0, concat_axis=0, tiled=True)  111 us
    pallas_call x1, Pallas kernels, contract(): pl.pallas_call(contract_kernel, out_shape=jax.ShapeDtypeStruct((HALF, 2 *...  15.1 us
    pallas_call x1, Pallas kernels, pack(): pl.pallas_call(pack_kernel, out_shape=jax.ShapeDtypeStruct((targets, mu /...  6.19 us
    ppermute x3, starting transfers between devices, local(): lax.ppermute(own, 'orb', [(i, i ^ step) for i in range(orbs)])  4.22 us
  transfers between devices with their start and end apart: 4, of which 1 were waited for; matrix products, arithmetic and copies ran while one was open for 0% of the time, Pallas kernels for 4%

profile of v5, /device:TPU:1, one launch (start us, length us, event | category | flops | bytes accessed | tf_op | source)
XLA Modules:
  0.0 138.3 jit_solution(4085084225397714046)
XLA Ops:
  0.0 0.0 copy-start
  0.0 3.6 %collective-permute-start.2 = (bf16[32,128]{1,0:T(8,128)(2,1)}, bf16[32,128]{1,0:T(8,128)(2,1)S(1)}, u32[]{:S(2)}, u32[]{:S(2)}) collective-permute-start(bf16[32,128]{1,0:T(8,128)(2,1)} %bitcast.1), channel_id=1, source_target_pairs={{0,3},{1,2},{2,1},{3,0},{4,7},{5,6},{6,5},{7,4},{8,11},{9,10},{10,... | collective-permute-start | bytes 24584 | tf_op jit(solution)/shard_map/ppermute | solution.py:147
  3.6 0.3 collective-permute-start.1
  3.9 0.3 collective-permute-start
  4.2 6.2 %shard_map.46.refs_4_ = bf16[32,68,16,128]{3,2,1,0:T(8,128)(2,1)S(1)} custom-call(bf16[128,16,2048]{2,1,0:T(8,128)(2,1)} %x_ref.1), custom_call_target="tpu_custom_call" | custom-call | bytes 16777216 | tf_op jit(solution)/shard_map/pallas_call | solution.py:36
  10.4 0.0 collective-permute-done.2.refs_3_
  10.4 0.0 collective-permute-done.1.refs_2_
  10.4 0.0 collective-permute-done.refs_1_
  10.5 0.0 copy-done
  10.5 0.1 shard_map.47
  10.6 0.0 copy-start.1
  10.6 0.0 copy-start.2
  10.6 110.6 %all_to_all.5.x_ref.mine_ref = bf16[32,68,16,128]{3,2,1,0:T(8,128)(2,1)S(1)} all-to-all(bf16[32,68,16,128]{3,2,1,0:T(8,128)(2,1)S(1)} %shard_map.47), channel_id=1, replica_groups=mesh['aux'=32,'orb'=4] {'aux'}, dimensions={0} | all-to-all | bytes 17825792 | tf_op jit(solution)/shard_map/all_to_all | solution.py:150
  121.3 0.1 collective-permute-start.3
  121.3 1.9 %collective-permute-done.3.other_ref = bf16[32,4,16,128]{3,2,1,0:T(8,128)(2,1)S(1)} collective-permute-done((bf16[32,4,16,128]{3,2,1,0:T(8,128)(2,1)S(1)}, bf16[32,4,16,128]{3,2,1,0:T(8,128)(2,1)S(1)}, u32[]{:S(2)}, u32[]{:S(2)}) %collective-permute-start.3) | collective-permute-done | bytes 524320 | tf_op jit(solution)/shard_map/ppermute | solution.py:151
  123.2 0.0 copy-done.1
  123.2 0.0 copy-done.2
  123.3 15.1 %shard_map.48 = bf16[64,128,1024]{2,1,0:T(8,128)(2,1)} custom-call(s32[4,4]{1,0:T(4,128)S(1)} %copy-done.1, s32[4,16]{1,0:T(4,128)S(1)} %copy-done.2, bf16[32,68,16,128]{3,2,1,0:T(8,128)(2,1)S(1)} %all_to_all.5.x_ref.mine_ref, bf16[32,68,16,128]{3,2,1,0:T(8,128)(2,1)S(1)} %all_to_all.5.x_ref.mine_ref, ...), custom_call_target="tpu_custom_call" | custom-call | flops 8589934592 | bytes 27262976 | tf_op jit(solution)/shard_map/pallas_call | solution.py:120
  (1 shorter events, 0.0 us)
Async XLA Ops:
  0.0 10.5 %copy-start = (bf16[128,32]{0,1:T(8,128)(2,1)S(1)}, bf16[128,32]{0,1:T(8,128)(2,1)}, u32[]{:S(2)}) copy-start(bf16[128,32]{0,1:T(8,128)(2,1)} %param.7) | copy-start | bytes 24580
  0.0 10.4 %collective-permute-start.2 = (bf16[32,128]{1,0:T(8,128)(2,1)}, bf16[32,128]{1,0:T(8,128)(2,1)S(1)}, u32[]{:S(2)}, u32[]{:S(2)}) collective-permute-start(bf16[32,128]{1,0:T(8,128)(2,1)} %bitcast.1), channel_id=1, source_target_pairs={{0,3},{1,2},{2,1},{3,0},{4,7},{5,6},{6,5},{7,4},{8,11},{9,10},{10,... | collective-permute-start | bytes 24584 | tf_op jit(solution)/shard_map/ppermute | solution.py:147
  3.6 6.9 %collective-permute-start.1 = (bf16[32,128]{1,0:T(8,128)(2,1)}, bf16[32,128]{1,0:T(8,128)(2,1)S(1)}, u32[]{:S(2)}, u32[]{:S(2)}) collective-permute-start(bf16[32,128]{1,0:T(8,128)(2,1)} %bitcast.2), channel_id=1, source_target_pairs={{0,2},{1,3},{2,0},{3,1},{4,6},{5,7},{6,4},{7,5},{8,10},{9,11},{10,... | collective-permute-start | bytes 24584 | tf_op jit(solution)/shard_map/ppermute | solution.py:147
  3.9 6.5 %collective-permute-start = (bf16[32,128]{1,0:T(8,128)(2,1)}, bf16[32,128]{1,0:T(8,128)(2,1)S(1)}, u32[]{:S(2)}, u32[]{:S(2)}) collective-permute-start(bf16[32,128]{1,0:T(8,128)(2,1)} %bitcast.3), channel_id=1, source_target_pairs={{0,1},{1,0},{2,3},{3,2},{4,5},{5,4},{6,7},{7,6},{8,9},{9,8},{10,11... | collective-permute-start | bytes 24584 | tf_op jit(solution)/shard_map/ppermute | solution.py:147
  10.6 112.7 %copy-start.1 = (s32[4,4]{1,0:T(4,128)S(1)}, s32[4,4]{1,0:T(4,128)}, u32[]{:S(2)}) copy-start(s32[4,4]{1,0:T(4,128)} %pair_ref.1) | copy-start | bytes 196
  10.6 112.7 %copy-start.2 = (s32[4,16]{1,0:T(4,128)S(1)}, s32[4,16]{1,0:T(4,128)}, u32[]{:S(2)}) copy-start(s32[4,16]{1,0:T(4,128)} %aux_ref.1) | copy-start | bytes 772
  121.3 2.0 %collective-permute-start.3 = (bf16[32,4,16,128]{3,2,1,0:T(8,128)(2,1)S(1)}, bf16[32,4,16,128]{3,2,1,0:T(8,128)(2,1)S(1)}, u32[]{:S(2)}, u32[]{:S(2)}) collective-permute-start(bf16[32,4,16,128]{3,2,1,0:T(8,128)(2,1)S(1)} %slice.4), channel_id=1, source_target_pairs={{0,4},{4,0},{8,12},{12,8},{16,20},{20,16},{24,28},{28,24},{32,36},... | collective-permute-start | bytes 1572872 | tf_op jit(solution)/shard_map/ppermute | solution.py:151

commit v6 on v5

--- a/solution.py
+++ b/solution.py
@@ -12,39 +12,39 @@
 PAIRS = 8
 SUBS = 2
 PITCH = 24
-VMEM = 60 << 20
 
 
-def pack_kernel(x_ref, *rest):
-    o_ref = rest[-1]
-    for group in range(x_ref.shape[0] // GROUP):
+def pack_kernel(x_ref, o_ref, held_ref, sems):
+    groups = x_ref.shape[0] // GROUP
+
+    def fetch(group):
+        rows = pl.ds(group * GROUP, GROUP)
+        return pltpu.make_async_copy(x_ref.at[rows], held_ref.at[rows], sems.at[group])
+
+    for group in range(groups):
+        fetch(group).start()
+    for group in range(groups):
+        fetch(group).wait()
         top = group * GROUP
         for block in range(x_ref.shape[2] // LANES):
             lanes = slice(block * LANES, (block + 1) * LANES)
-            low, high = x_ref[top : top + PAIRS, :, lanes], x_ref[top + PAIRS : top + GROUP, :, lanes]
+            low, high = held_ref[top : top + PAIRS, :, lanes], held_ref[top + PAIRS : top + GROUP, :, lanes]
             rows = slice(group * PAIRS, (group + 1) * PAIRS)
             o_ref[2 * block, rows] = jnp.concatenate([low[..., :HALF], high[..., :HALF]], axis=-1)
             o_ref[2 * block + 1, rows] = jnp.concatenate([low[..., HALF:], high[..., HALF:]], axis=-1)
 
 
-def pack(three_centre, first, count, rows, extra, earlier=None):
+def pack(three_centre, extra):
     mu, nu, p_total = three_centre.shape
-    targets = p_total // HALF
-    args, specs, aliases = [pltpu.with_memory_space_constraint(three_centre, pltpu.HBM)], [pl.BlockSpec((rows, nu, p_total), lambda i: (first + i, 0, 0))], {}
-    if earlier is not None:
-        args, specs, aliases = args + [earlier], specs + [pl.BlockSpec(memory_space=pl.ANY)], {1: 0}
     return pl.pallas_call(
         pack_kernel,
-        out_shape=jax.ShapeDtypeStruct((targets, mu // 2 + extra, nu, LANES), jnp.bfloat16),
-        grid=(count,),
-        in_specs=specs,
-        out_specs=pl.BlockSpec((targets, rows // 2, nu, LANES), lambda i: (0, first + i, 0, 0)),
-        input_output_aliases=aliases,
+        out_shape=pltpu.VMEM((p_total // HALF, mu // 2 + extra, nu, LANES), jnp.bfloat16),
+        in_specs=[pl.BlockSpec(memory_space=pl.ANY)],
+        out_specs=pl.BlockSpec(memory_space=pltpu.VMEM),
+        scratch_shapes=[pltpu.VMEM(three_centre.shape, jnp.bfloat16), pltpu.SemaphoreType.DMA((mu // GROUP,))],
         compiler_params=pltpu.CompilerParams(vmem_limit_bytes=36 << 20),
-        cost_estimate=pl.CostEstimate(
-            flops=0, bytes_accessed=4 * count * rows * nu * p_total, transcendentals=0
-        ),
-    )(*args)
+        cost_estimate=pl.CostEstimate(flops=0, bytes_accessed=4 * mu * nu * p_total, transcendentals=0),
+    )(pltpu.with_memory_space_constraint(three_centre, pltpu.HBM))
 
 
 def append_kernel(*refs):
@@ -145,7 +145,7 @@
     aux_count, orbs = lax.axis_size("aux"), lax.axis_size("orb")
     own = density.T
     others = [lax.ppermute(own, "orb", [(i, i ^ step) for i in range(orbs)]) for step in range(1, orbs)]
-    sent = pack(three_centre, 0, mu // 64, 64, orbs)
+    sent = pack(three_centre, orbs)
     sent = append(sent, (own, *others))
     moved = lax.all_to_all(sent, "aux", split_axis=0, concat_axis=0, tiled=True)
     other = lax.ppermute(moved[:, mu // 2 :], "aux", [(i, i ^ 1) for i in range(aux_count)])

time: 138 us -> 137 us (level)
  Pallas kernels: 21.4 us -> 19.2 us
    pallas_call x1, Pallas kernels: 6.19 us -> 4.02 us  [pack(): pl.pallas_call(pack_kernel, out_shape=pltpu.VMEM((p_total // HALF, mu //...]
  transfers between devices with their start and end apart: 4 -> 4, of which waited for: 1 -> 1; matrix products, arithmetic and copies ran while one was open for 0% -> 0% of each run, Pallas kernels for 4% -> 3%
where the time goes in v6:
time: 137 us; the launch traced here: 136 us
  blocking collectives  111 us (81%)
  Pallas kernels  19.2 us (14%)
  starting transfers between devices  4.3 us (3%)
  waiting for transfers between devices  1.9 us (1%)
    all_to_all x1, blocking collectives, local(): moved = lax.all_to_all(sent, 'aux', split_axis=0, concat_axis=0, tiled=True)  111 us
    pallas_call x1, Pallas kernels, contract(): pl.pallas_call(contract_kernel, out_shape=jax.ShapeDtypeStruct((HALF, 2 *...  15.1 us
    ppermute x3, starting transfers between devices, local(): lax.ppermute(own, 'orb', [(i, i ^ step) for i in range(orbs)])  4.22 us
    pallas_call x1, Pallas kernels, pack(): pl.pallas_call(pack_kernel, out_shape=pltpu.VMEM((p_total // HALF, mu //...  4.02 us
  transfers between devices with their start and end apart: 4, of which 1 were waited for; matrix products, arithmetic and copies ran while one was open for 0% of the time, Pallas kernels for 3%

profile of v6, /device:TPU:1, one launch (start us, length us, event | category | flops | bytes accessed | tf_op | source)
XLA Modules:
  0.0 136.4 jit_solution(8932649616281486977)
XLA Ops:
  0.0 0.0 copy-start
  0.0 3.6 %collective-permute-start.2 = (bf16[32,128]{1,0:T(8,128)(2,1)}, bf16[32,128]{1,0:T(8,128)(2,1)S(1)}, u32[]{:S(2)}, u32[]{:S(2)}) collective-permute-start(bf16[32,128]{1,0:T(8,128)(2,1)} %bitcast.1), channel_id=1, source_target_pairs={{0,3},{1,2},{2,1},{3,0},{4,7},{5,6},{6,5},{7,4},{8,11},{9,10},{10,... | collective-permute-start | bytes 24584 | tf_op jit(solution)/shard_map/ppermute | solution.py:147
  3.6 0.3 collective-permute-start.1
  3.9 0.3 collective-permute-start
  4.2 4.0 %shard_map.46.refs_4_ = bf16[32,68,16,128]{3,2,1,0:T(8,128)(2,1)S(1)} custom-call(bf16[128,16,2048]{2,1,0:T(8,128)(2,1)} %x_ref.1), custom_call_target="tpu_custom_call" | custom-call | bytes 16777216 | tf_op jit(solution)/shard_map/pallas_call | solution.py:39
  8.3 0.0 collective-permute-done.2.refs_3_
  8.3 0.0 collective-permute-done.1.refs_2_
  8.3 0.0 collective-permute-done.refs_1_
  8.3 0.0 copy-done
  8.3 0.1 shard_map.47
  8.4 0.0 copy-start.1
  8.4 0.0 copy-start.2
  8.4 110.8 %all_to_all.5.x_ref.mine_ref = bf16[32,68,16,128]{3,2,1,0:T(8,128)(2,1)S(1)} all-to-all(bf16[32,68,16,128]{3,2,1,0:T(8,128)(2,1)S(1)} %shard_map.47), channel_id=1, replica_groups=mesh['aux'=32,'orb'=4] {'aux'}, dimensions={0} | all-to-all | bytes 17825792 | tf_op jit(solution)/shard_map/all_to_all | solution.py:150
  119.3 0.1 collective-permute-start.3
  119.4 1.9 %collective-permute-done.3.other_ref = bf16[32,4,16,128]{3,2,1,0:T(8,128)(2,1)S(1)} collective-permute-done((bf16[32,4,16,128]{3,2,1,0:T(8,128)(2,1)S(1)}, bf16[32,4,16,128]{3,2,1,0:T(8,128)(2,1)S(1)}, u32[]{:S(2)}, u32[]{:S(2)}) %collective-permute-start.3) | collective-permute-done | bytes 524320 | tf_op jit(solution)/shard_map/ppermute | solution.py:151
  121.3 0.0 copy-done.1
  121.3 0.0 copy-done.2
  121.3 15.1 %shard_map.48 = bf16[64,128,1024]{2,1,0:T(8,128)(2,1)} custom-call(s32[4,4]{1,0:T(4,128)S(1)} %copy-done.1, s32[4,16]{1,0:T(4,128)S(1)} %copy-done.2, bf16[32,68,16,128]{3,2,1,0:T(8,128)(2,1)S(1)} %all_to_all.5.x_ref.mine_ref, bf16[32,68,16,128]{3,2,1,0:T(8,128)(2,1)S(1)} %all_to_all.5.x_ref.mine_ref, ...), custom_call_target="tpu_custom_call" | custom-call | flops 8589934592 | bytes 27262976 | tf_op jit(solution)/shard_map/pallas_call | solution.py:120
  (1 shorter events, 0.0 us)
Async XLA Ops:
  0.0 8.3 %copy-start = (bf16[128,32]{0,1:T(8,128)(2,1)S(1)}, bf16[128,32]{0,1:T(8,128)(2,1)}, u32[]{:S(2)}) copy-start(bf16[128,32]{0,1:T(8,128)(2,1)} %param.7) | copy-start | bytes 24580
  0.0 8.3 %collective-permute-start.2 = (bf16[32,128]{1,0:T(8,128)(2,1)}, bf16[32,128]{1,0:T(8,128)(2,1)S(1)}, u32[]{:S(2)}, u32[]{:S(2)}) collective-permute-start(bf16[32,128]{1,0:T(8,128)(2,1)} %bitcast.1), channel_id=1, source_target_pairs={{0,3},{1,2},{2,1},{3,0},{4,7},{5,6},{6,5},{7,4},{8,11},{9,10},{10,... | collective-permute-start | bytes 24584 | tf_op jit(solution)/shard_map/ppermute | solution.py:147
  3.6 4.7 %collective-permute-start.1 = (bf16[32,128]{1,0:T(8,128)(2,1)}, bf16[32,128]{1,0:T(8,128)(2,1)S(1)}, u32[]{:S(2)}, u32[]{:S(2)}) collective-permute-start(bf16[32,128]{1,0:T(8,128)(2,1)} %bitcast.2), channel_id=1, source_target_pairs={{0,2},{1,3},{2,0},{3,1},{4,6},{5,7},{6,4},{7,5},{8,10},{9,11},{10,... | collective-permute-start | bytes 24584 | tf_op jit(solution)/shard_map/ppermute | solution.py:147
  3.9 4.4 %collective-permute-start = (bf16[32,128]{1,0:T(8,128)(2,1)}, bf16[32,128]{1,0:T(8,128)(2,1)S(1)}, u32[]{:S(2)}, u32[]{:S(2)}) collective-permute-start(bf16[32,128]{1,0:T(8,128)(2,1)} %bitcast.3), channel_id=1, source_target_pairs={{0,1},{1,0},{2,3},{3,2},{4,5},{5,4},{6,7},{7,6},{8,9},{9,8},{10,11... | collective-permute-start | bytes 24584 | tf_op jit(solution)/shard_map/ppermute | solution.py:147
  8.4 112.9 %copy-start.1 = (s32[4,4]{1,0:T(4,128)S(1)}, s32[4,4]{1,0:T(4,128)}, u32[]{:S(2)}) copy-start(s32[4,4]{1,0:T(4,128)} %pair_ref.1) | copy-start | bytes 196
  8.4 112.9 %copy-start.2 = (s32[4,16]{1,0:T(4,128)S(1)}, s32[4,16]{1,0:T(4,128)}, u32[]{:S(2)}) copy-start(s32[4,16]{1,0:T(4,128)} %aux_ref.1) | copy-start | bytes 772
  119.3 2.0 %collective-permute-start.3 = (bf16[32,4,16,128]{3,2,1,0:T(8,128)(2,1)S(1)}, bf16[32,4,16,128]{3,2,1,0:T(8,128)(2,1)S(1)}, u32[]{:S(2)}, u32[]{:S(2)}) collective-permute-start(bf16[32,4,16,128]{3,2,1,0:T(8,128)(2,1)S(1)} %slice.4), channel_id=1, source_target_pairs={{0,4},{4,0},{8,12},{12,8},{16,20},{20,16},{24,28},{28,24},{32,36},... | collective-permute-start | bytes 1572872 | tf_op jit(solution)/shard_map/ppermute | solution.py:151

commit v7 on v6

--- a/solution.py
+++ b/solution.py
@@ -72,10 +72,12 @@
     )(*parts, sent)
 
 
-def contract_kernel(pair_ref, aux_ref, x_ref, mine_ref, other_ref, o_ref, dens_ref, rows_ref):
+def contract_kernel(pair_ref, aux_ref, x_ref, other_ref, o_ref, dens_ref, rows_ref):
     sources, _, nu, _ = x_ref.shape
     depth = sources * nu
-    _, orbs, half, lanes = mine_ref.shape
+    _, orbs, half, lanes = other_ref.shape
+    behind = x_ref.shape[1] - orbs
+    first = pl.program_id(0) * SUBS * PAIRS
     aux_pos, orb_pos = lax.axis_index("aux"), lax.axis_index("orb")
 
     @pl.when(pl.program_id(0) == 0)
@@ -84,13 +86,13 @@
         column = lax.div(aux_pos * HALF, BLK)
         for orb in range(orbs):
             keep = (pair_ref[orb_pos, orb] * aux_ref[orb, column]).astype(jnp.float32).astype(jnp.bfloat16)
-            mine, other = mine_ref[:, orb], other_ref[:, orb]
+            mine, other = x_ref[:, behind + orb], other_ref[:, orb]
             low, high = jnp.where(upper, other, mine), jnp.where(upper, mine, other)
             whole = jnp.stack([low, high], axis=1).reshape(sources * 2 * half, lanes)
             dens_ref[orb * lanes : (orb + 1) * lanes, :] = whole.T * keep
 
     def order_rows(sub, pair):
-        turned = x_ref[:, sub * PAIRS + pair].reshape(depth, LANES).T.astype(jnp.float32)
+        turned = x_ref[:, first + sub * PAIRS + pair].reshape(depth, LANES).T.astype(jnp.float32)
         for k in range(depth // LANES):
             piece = turned[:, k * LANES : (k + 1) * LANES]
             base = k * HALF * PITCH + pair
@@ -124,8 +126,7 @@
         in_specs=[
             pl.BlockSpec(memory_space=pltpu.SMEM),
             pl.BlockSpec(memory_space=pltpu.SMEM),
-            pl.BlockSpec((sources, SUBS * PAIRS, nu, LANES), lambda i: (0, i, 0, 0)),
-            pl.BlockSpec((sources, orbs, nu, LANES), lambda i: (0, pairs // orbs, 0, 0)),
+            pl.BlockSpec(memory_space=pltpu.VMEM),
             pl.BlockSpec(other.shape, lambda i: (0, 0, 0, 0)),
         ],
         out_specs=pl.BlockSpec((HALF, SUBS * GROUP, sig), lambda i: (0, i, 0)),
@@ -137,7 +138,7 @@
         cost_estimate=pl.CostEstimate(
             flops=4 * HALF * pairs * orbs * LANES * sig, bytes_accessed=26 << 20, transcendentals=0
         ),
-    )(pair_mask, aux_mask, moved, moved, other)
+    )(pair_mask, aux_mask, pltpu.with_memory_space_constraint(moved, pltpu.VMEM), other)
 
 
 def local(three_centre, pair_mask, aux_mask, density):

time: 137 us -> 135 us (0.985)
  no operation moved by 1% of the time
where the time goes in v7:
time: 135 us
  blocking collectives  111 us (82%)
  Pallas kernels  18 us (13%)
  starting transfers between devices  4.3 us (3%)
  waiting for transfers between devices  1.9 us (1%)
    all_to_all x1, blocking collectives, local(): moved = lax.all_to_all(sent, 'aux', split_axis=0, concat_axis=0, tiled=True)  111 us
    pallas_call x1, Pallas kernels, contract(): pl.pallas_call(contract_kernel, out_shape=jax.ShapeDtypeStruct((HALF, 2 *...  13.9 us
    ppermute x3, starting transfers between devices, local(): lax.ppermute(own, 'orb', [(i, i ^ step) for i in range(orbs)])  4.22 us
    pallas_call x1, Pallas kernels, pack(): pl.pallas_call(pack_kernel, out_shape=pltpu.VMEM((p_total // HALF, mu //...  4.02 us
  transfers between devices with their start and end apart: 4, of which 1 were waited for; matrix products, arithmetic and copies ran while one was open for 0% of the time, Pallas kernels for 3%

profile of v7, /device:TPU:1, one launch (start us, length us, event | category | flops | bytes accessed | tf_op | source)
XLA Modules:
  0.0 135.2 jit_solution(1017967477526196687)
XLA Ops:
  0.0 0.0 copy-start
  0.0 3.6 %collective-permute-start.2 = (bf16[32,128]{1,0:T(8,128)(2,1)}, bf16[32,128]{1,0:T(8,128)(2,1)S(1)}, u32[]{:S(2)}, u32[]{:S(2)}) collective-permute-start(bf16[32,128]{1,0:T(8,128)(2,1)} %bitcast.1), channel_id=1, source_target_pairs={{0,3},{1,2},{2,1},{3,0},{4,7},{5,6},{6,5},{7,4},{8,11},{9,10},{10,... | collective-permute-start | bytes 24584 | tf_op jit(solution)/shard_map/ppermute | solution.py:148
  3.6 0.3 collective-permute-start.1
  3.9 0.3 collective-permute-start
  4.2 4.0 %shard_map.46.refs_4_ = bf16[32,68,16,128]{3,2,1,0:T(8,128)(2,1)S(1)} custom-call(bf16[128,16,2048]{2,1,0:T(8,128)(2,1)} %x_ref.1), custom_call_target="tpu_custom_call" | custom-call | bytes 16777216 | tf_op jit(solution)/shard_map/pallas_call | solution.py:39
  8.3 0.0 collective-permute-done.2.refs_3_
  8.3 0.0 collective-permute-done.1.refs_2_
  8.3 0.0 collective-permute-done.refs_1_
  8.3 0.0 copy-done
  8.3 0.1 shard_map.47
  8.4 0.0 copy-start.1
  8.4 0.0 copy-start.2
  8.4 110.8 %all_to_all.5.x_ref = bf16[32,68,16,128]{3,2,1,0:T(8,128)(2,1)S(1)} all-to-all(bf16[32,68,16,128]{3,2,1,0:T(8,128)(2,1)S(1)} %shard_map.47), channel_id=1, replica_groups=mesh['aux'=32,'orb'=4] {'aux'}, dimensions={0} | all-to-all | bytes 17825792 | tf_op jit(solution)/shard_map/all_to_all | solution.py:151
  119.3 0.1 collective-permute-start.3
  119.4 1.9 %collective-permute-done.3.other_ref = bf16[32,4,16,128]{3,2,1,0:T(8,128)(2,1)S(1)} collective-permute-done((bf16[32,4,16,128]{3,2,1,0:T(8,128)(2,1)S(1)}, bf16[32,4,16,128]{3,2,1,0:T(8,128)(2,1)S(1)}, u32[]{:S(2)}, u32[]{:S(2)}) %collective-permute-start.3) | collective-permute-done | bytes 524320 | tf_op jit(solution)/shard_map/ppermute | solution.py:152
  121.3 0.0 copy-done.1
  121.3 0.0 copy-done.2
  121.3 13.9 %shard_map.48 = bf16[64,128,1024]{2,1,0:T(8,128)(2,1)} custom-call(s32[4,4]{1,0:T(4,128)S(1)} %copy-done.1, s32[4,16]{1,0:T(4,128)S(1)} %copy-done.2, bf16[32,68,16,128]{3,2,1,0:T(8,128)(2,1)S(1)} %all_to_all.5.x_ref, bf16[32,4,16,128]{3,2,1,0:T(8,128)(2,1)S(1)} %collective-permute-done.3.other_ref), custom_call_target="tpu_custom_call" | custom-call | flops 8589934592 | bytes 27262976 | tf_op jit(solution)/shard_map/pallas_call | solution.py:122
  (1 shorter events, 0.0 us)
Async XLA Ops:
  0.0 8.3 %copy-start = (bf16[128,32]{0,1:T(8,128)(2,1)S(1)}, bf16[128,32]{0,1:T(8,128)(2,1)}, u32[]{:S(2)}) copy-start(bf16[128,32]{0,1:T(8,128)(2,1)} %param.7) | copy-start | bytes 24580
  0.0 8.3 %collective-permute-start.2 = (bf16[32,128]{1,0:T(8,128)(2,1)}, bf16[32,128]{1,0:T(8,128)(2,1)S(1)}, u32[]{:S(2)}, u32[]{:S(2)}) collective-permute-start(bf16[32,128]{1,0:T(8,128)(2,1)} %bitcast.1), channel_id=1, source_target_pairs={{0,3},{1,2},{2,1},{3,0},{4,7},{5,6},{6,5},{7,4},{8,11},{9,10},{10,... | collective-permute-start | bytes 24584 | tf_op jit(solution)/shard_map/ppermute | solution.py:148
  3.6 4.7 %collective-permute-start.1 = (bf16[32,128]{1,0:T(8,128)(2,1)}, bf16[32,128]{1,0:T(8,128)(2,1)S(1)}, u32[]{:S(2)}, u32[]{:S(2)}) collective-permute-start(bf16[32,128]{1,0:T(8,128)(2,1)} %bitcast.2), channel_id=1, source_target_pairs={{0,2},{1,3},{2,0},{3,1},{4,6},{5,7},{6,4},{7,5},{8,10},{9,11},{10,... | collective-permute-start | bytes 24584 | tf_op jit(solution)/shard_map/ppermute | solution.py:148
  3.9 4.4 %collective-permute-start = (bf16[32,128]{1,0:T(8,128)(2,1)}, bf16[32,128]{1,0:T(8,128)(2,1)S(1)}, u32[]{:S(2)}, u32[]{:S(2)}) collective-permute-start(bf16[32,128]{1,0:T(8,128)(2,1)} %bitcast.3), channel_id=1, source_target_pairs={{0,1},{1,0},{2,3},{3,2},{4,5},{5,4},{6,7},{7,6},{8,9},{9,8},{10,11... | collective-permute-start | bytes 24584 | tf_op jit(solution)/shard_map/ppermute | solution.py:148
  8.4 112.9 %copy-start.1 = (s32[4,4]{1,0:T(4,128)S(1)}, s32[4,4]{1,0:T(4,128)}, u32[]{:S(2)}) copy-start(s32[4,4]{1,0:T(4,128)} %pair_ref.1) | copy-start | bytes 196
  8.4 112.9 %copy-start.2 = (s32[4,16]{1,0:T(4,128)S(1)}, s32[4,16]{1,0:T(4,128)}, u32[]{:S(2)}) copy-start(s32[4,16]{1,0:T(4,128)} %aux_ref.1) | copy-start | bytes 772
  119.3 2.0 %collective-permute-start.3 = (bf16[32,4,16,128]{3,2,1,0:T(8,128)(2,1)S(1)}, bf16[32,4,16,128]{3,2,1,0:T(8,128)(2,1)S(1)}, u32[]{:S(2)}, u32[]{:S(2)}) collective-permute-start(bf16[32,4,16,128]{3,2,1,0:T(8,128)(2,1)S(1)} %slice.4), channel_id=1, source_target_pairs={{0,4},{4,0},{8,12},{12,8},{16,20},{20,16},{24,28},{28,24},{32,36},... | collective-permute-start | bytes 1572872 | tf_op jit(solution)/shard_map/ppermute | solution.py:152

commit v8 on v7

--- a/solution.py
+++ b/solution.py
@@ -10,7 +10,7 @@
 HALF = 64
 GROUP = 16
 PAIRS = 8
-SUBS = 2
+SUBS = 1
 PITCH = 24
 
 

time: 135 us -> 136 us (level)
  no operation moved by 1% of the time
where the time goes in v8:
time: 136 us
  blocking collectives  111 us (82%)
  Pallas kernels  18.9 us (14%)
  starting transfers between devices  4.3 us (3%)
  waiting for transfers between devices  1.9 us (1%)
    all_to_all x1, blocking collectives, local(): moved = lax.all_to_all(sent, 'aux', split_axis=0, concat_axis=0, tiled=True)  111 us
    pallas_call x1, Pallas kernels, contract(): pl.pallas_call(contract_kernel, out_shape=jax.ShapeDtypeStruct((HALF, 2 *...  14.8 us
    ppermute x3, starting transfers between devices, local(): lax.ppermute(own, 'orb', [(i, i ^ step) for i in range(orbs)])  4.22 us
    pallas_call x1, Pallas kernels, pack(): pl.pallas_call(pack_kernel, out_shape=pltpu.VMEM((p_total // HALF, mu //...  4.02 us
  transfers between devices with their start and end apart: 4, of which 1 were waited for; matrix products, arithmetic and copies ran while one was open for 0% of the time, Pallas kernels for 3%

profile of v8, /device:TPU:1, one launch (start us, length us, event | category | flops | bytes accessed | tf_op | source)
XLA Modules:
  0.0 136.1 jit_solution(13080613436046049884)
XLA Ops:
  0.0 0.0 copy-start
  0.0 3.6 %collective-permute-start.2 = (bf16[32,128]{1,0:T(8,128)(2,1)}, bf16[32,128]{1,0:T(8,128)(2,1)S(1)}, u32[]{:S(2)}, u32[]{:S(2)}) collective-permute-start(bf16[32,128]{1,0:T(8,128)(2,1)} %bitcast.1), channel_id=1, source_target_pairs={{0,3},{1,2},{2,1},{3,0},{4,7},{5,6},{6,5},{7,4},{8,11},{9,10},{10,... | collective-permute-start | bytes 24584 | tf_op jit(solution)/shard_map/ppermute | solution.py:148
  3.6 0.3 collective-permute-start.1
  3.9 0.3 collective-permute-start
  4.2 4.0 %shard_map.46.refs_4_ = bf16[32,68,16,128]{3,2,1,0:T(8,128)(2,1)S(1)} custom-call(bf16[128,16,2048]{2,1,0:T(8,128)(2,1)} %x_ref.1), custom_call_target="tpu_custom_call" | custom-call | bytes 16777216 | tf_op jit(solution)/shard_map/pallas_call | solution.py:39
  8.3 0.0 collective-permute-done.2.refs_3_
  8.3 0.0 collective-permute-done.1.refs_2_
  8.3 0.0 collective-permute-done.refs_1_
  8.3 0.0 copy-done
  8.3 0.1 shard_map.47
  8.4 0.0 copy-start.1
  8.4 0.0 copy-start.2
  8.4 110.8 %all_to_all.5.x_ref = bf16[32,68,16,128]{3,2,1,0:T(8,128)(2,1)S(1)} all-to-all(bf16[32,68,16,128]{3,2,1,0:T(8,128)(2,1)S(1)} %shard_map.47), channel_id=1, replica_groups=mesh['aux'=32,'orb'=4] {'aux'}, dimensions={0} | all-to-all | bytes 17825792 | tf_op jit(solution)/shard_map/all_to_all | solution.py:151
  119.3 0.1 collective-permute-start.3
  119.4 1.9 %collective-permute-done.3.other_ref = bf16[32,4,16,128]{3,2,1,0:T(8,128)(2,1)S(1)} collective-permute-done((bf16[32,4,16,128]{3,2,1,0:T(8,128)(2,1)S(1)}, bf16[32,4,16,128]{3,2,1,0:T(8,128)(2,1)S(1)}, u32[]{:S(2)}, u32[]{:S(2)}) %collective-permute-start.3) | collective-permute-done | bytes 524320 | tf_op jit(solution)/shard_map/ppermute | solution.py:152
  121.3 0.0 copy-done.1
  121.3 0.0 copy-done.2
  121.3 14.8 %shard_map.48 = bf16[64,128,1024]{2,1,0:T(8,128)(2,1)} custom-call(s32[4,4]{1,0:T(4,128)S(1)} %copy-done.1, s32[4,16]{1,0:T(4,128)S(1)} %copy-done.2, bf16[32,68,16,128]{3,2,1,0:T(8,128)(2,1)S(1)} %all_to_all.5.x_ref, bf16[32,4,16,128]{3,2,1,0:T(8,128)(2,1)S(1)} %collective-permute-done.3.other_ref), custom_call_target="tpu_custom_call" | custom-call | flops 8589934592 | bytes 27262976 | tf_op jit(solution)/shard_map/pallas_call | solution.py:122
  (1 shorter events, 0.0 us)
Async XLA Ops:
  0.0 8.3 %copy-start = (bf16[128,32]{0,1:T(8,128)(2,1)S(1)}, bf16[128,32]{0,1:T(8,128)(2,1)}, u32[]{:S(2)}) copy-start(bf16[128,32]{0,1:T(8,128)(2,1)} %param.7) | copy-start | bytes 24580
  0.0 8.3 %collective-permute-start.2 = (bf16[32,128]{1,0:T(8,128)(2,1)}, bf16[32,128]{1,0:T(8,128)(2,1)S(1)}, u32[]{:S(2)}, u32[]{:S(2)}) collective-permute-start(bf16[32,128]{1,0:T(8,128)(2,1)} %bitcast.1), channel_id=1, source_target_pairs={{0,3},{1,2},{2,1},{3,0},{4,7},{5,6},{6,5},{7,4},{8,11},{9,10},{10,... | collective-permute-start | bytes 24584 | tf_op jit(solution)/shard_map/ppermute | solution.py:148
  3.6 4.7 %collective-permute-start.1 = (bf16[32,128]{1,0:T(8,128)(2,1)}, bf16[32,128]{1,0:T(8,128)(2,1)S(1)}, u32[]{:S(2)}, u32[]{:S(2)}) collective-permute-start(bf16[32,128]{1,0:T(8,128)(2,1)} %bitcast.2), channel_id=1, source_target_pairs={{0,2},{1,3},{2,0},{3,1},{4,6},{5,7},{6,4},{7,5},{8,10},{9,11},{10,... | collective-permute-start | bytes 24584 | tf_op jit(solution)/shard_map/ppermute | solution.py:148
  3.9 4.4 %collective-permute-start = (bf16[32,128]{1,0:T(8,128)(2,1)}, bf16[32,128]{1,0:T(8,128)(2,1)S(1)}, u32[]{:S(2)}, u32[]{:S(2)}) collective-permute-start(bf16[32,128]{1,0:T(8,128)(2,1)} %bitcast.3), channel_id=1, source_target_pairs={{0,1},{1,0},{2,3},{3,2},{4,5},{5,4},{6,7},{7,6},{8,9},{9,8},{10,11... | collective-permute-start | bytes 24584 | tf_op jit(solution)/shard_map/ppermute | solution.py:148
  8.4 112.9 %copy-start.1 = (s32[4,4]{1,0:T(4,128)S(1)}, s32[4,4]{1,0:T(4,128)}, u32[]{:S(2)}) copy-start(s32[4,4]{1,0:T(4,128)} %pair_ref.1) | copy-start | bytes 196
  8.4 112.9 %copy-start.2 = (s32[4,16]{1,0:T(4,128)S(1)}, s32[4,16]{1,0:T(4,128)}, u32[]{:S(2)}) copy-start(s32[4,16]{1,0:T(4,128)} %aux_ref.1) | copy-start | bytes 772
  119.3 2.0 %collective-permute-start.3 = (bf16[32,4,16,128]{3,2,1,0:T(8,128)(2,1)S(1)}, bf16[32,4,16,128]{3,2,1,0:T(8,128)(2,1)S(1)}, u32[]{:S(2)}, u32[]{:S(2)}) collective-permute-start(bf16[32,4,16,128]{3,2,1,0:T(8,128)(2,1)S(1)} %slice.4), channel_id=1, source_target_pairs={{0,4},{4,0},{8,12},{12,8},{16,20},{20,16},{24,28},{28,24},{32,36},... | collective-permute-start | bytes 1572872 | tf_op jit(solution)/shard_map/ppermute | solution.py:152
